TPU v7x, 512 devices: a whole 4x4x16 slice. The times are simulated.
512 devices in a mesh: stretch: 16 (over z_hi, y, core), worker: 32 (over x, z_lo).
Axes of the slice: x: 4, y: 4, z: 16 (z_hi: 2, z_lo: 8; z = z_hi * 8 + z_lo), core: 2. Of those that a mesh axis runs over, the one named last changes fastest.
Arguments:
- theta: bfloat16 [16, 32, 3, 512, 512], P('stretch', None, None, 'worker'), may hold values from -6 to 6
- gates: float32 [16, 32, 3, 3], P('stretch'), may hold values from -3.5 to 3.5
- edge_weights: float32 [16, 32, 512], P('stretch', None, 'worker'), may hold values from 0.25 to 2
- sizes: int32 [16, 32], P('stretch'), may hold values from 64 to 512
- ranks: int32 [16, 32], P('stretch'), may hold values from 6 to 48
- order: int32 [16, 32], P('stretch'), may hold values from 0 to 31, each once within a row
- sketch: bfloat16 [16, 512, 48], P('stretch'), may hold values from -0.25 to 0.25
Outputs:
- factors: bfloat16 [16, 32, 48, 512], P('stretch', 'worker')
Inputs may be any that keep to these rules, and one draw needn't show every extreme that they name: Each row order[s, :] is a permutation of 0 to 31.
All inputs are finite; a program needn't handle non-finite values.
Results may differ from a plain program's by a relative error of at most 0.0053.
Values may be sent and summed in bfloat16 or wider, within the bound.
No kernel may reach another device: no remote copies, remote signals or barrier semaphores. Data moves between devices by JAX's collectives and lax.ppermute only.
A program may use at most 64 MiB of HBM per device.

v0:
```python
import jax
import jax.numpy as jnp
from jax import lax
from jax.sharding import PartitionSpec as P


def from_behind(shard, axis, by):
    count = lax.axis_size(axis)
    return lax.ppermute(shard, axis, [(i, (i + by) % count) for i in range(count)])


def body(theta, gates, edge_weights, sizes, ranks, order, sketch):
    nwork = lax.axis_size("worker")
    left_weights = from_behind(edge_weights[0], "stretch", 1)
    picks = order[0]
    local = theta[0][picks]
    mixers = gates[0][picks]
    weights = left_weights[picks]
    live_sizes = sizes[0][picks]
    wanted = ranks[0][picks]
    local_sketch = sketch[0]
    count = local.shape[0]
    rows = local.shape[2]
    width = local.shape[3]
    rank_cap = local_sketch.shape[1]
    owned_count = count // nwork
    first_row = lax.axis_index("worker") * rows
    mixed = mixers[:, :, 0, None, None] * local[:, None, 0].astype(jnp.float32)
    mixed = mixed + mixers[:, :, 1, None, None] * local[:, None, 1].astype(jnp.float32)
    mixed = mixed + mixers[:, :, 2, None, None] * local[:, None, 2].astype(jnp.float32)
    row_index = first_row + jnp.arange(rows, dtype=jnp.int32)
    row_live = (row_index[None, :] < live_sizes[:, None]).astype(jnp.float32)
    col_live = (jnp.arange(width, dtype=jnp.int32)[None, :] < live_sizes[:, None]).astype(
        jnp.float32
    )
    mixed = mixed * (row_live * weights)[:, None, :, None] * col_live[:, None, None, :]
    block_rows = mixed.astype(jnp.bfloat16)
    kept = jnp.minimum(wanted, live_sizes // 2)
    columns = (jnp.arange(rank_cap, dtype=jnp.int32)[None, :] < kept[:, None]).astype(jnp.float32)
    mine = lax.dynamic_slice_in_dim(columns, lax.axis_index("worker") * owned_count, owned_count, 0)
    flat = block_rows.reshape(count, 3 * rows, width)
    sample = jnp.einsum("nrb,bk->nrk", flat, local_sketch, preferred_element_type=jnp.float32)
    sample = (sample * columns[:, None, :]).astype(jnp.bfloat16)
    gram_part = jnp.einsum("nrk,nrl->nkl", sample, sample, preferred_element_type=jnp.float32)
    proj_part = jnp.einsum("nrk,nrb->nkb", sample, flat, preferred_element_type=jnp.float32)
    gram, projected = (
        lax.psum_scatter(gram_part, "worker", scatter_dimension=0, tiled=True),
        lax.psum_scatter(proj_part, "worker", scatter_dimension=0, tiled=True),
    )
    gram = gram + (1.0 - mine)[:, :, None] * jnp.eye(rank_cap, dtype=jnp.float32)[None]
    lower = jnp.linalg.cholesky(gram)
    right = jax.scipy.linalg.solve_triangular(lower, projected, lower=True)
    total = lax.psum(jnp.sum(right * right), "worker")
    scale = jnp.sqrt(jnp.float32(count) / total)
    return (right * scale).astype(jnp.bfloat16)[None]


def solution(mesh):
    return jax.shard_map(
        body,
        mesh=mesh,
        in_specs=(
            P("stretch", None, None, "worker", None),
            P("stretch", None, None, None),
            P("stretch", None, "worker"),
            P("stretch", None),
            P("stretch", None),
            P("stretch", None),
            P("stretch", None, None),
        ),
        out_specs=P("stretch", "worker", None, None),
        check_vma=False,
    )
```

profile of v0, /device:TPU:8, one launch (start us, length us, event | category | flops | bytes accessed | tf_op | source)
XLA Modules:
  0.0 640.8 jit_solution(13912166504673050088)
XLA Ops:
  6.5 0.0 copy-start
  6.5 0.9 copy.25
  7.4 1.9 collective-permute-start
  9.4 0.7 fusion.17
  10.0 1.4 gather_fusion.2
  11.4 0.1 fusion.11
  11.5 1.8 gather_fusion.1
  13.3 3.2 fusion.8
  16.4 0.1 copy.18
  16.5 0.6 gather_fusion
  17.2 0.0 copy-start.2
  17.2 0.1 fusion.19
  17.3 0.7 gather_fusion.4
  18.0 0.1 fusion.16
  18.1 0.1 copy.23
  18.2 0.1 copy.24
  18.3 0.1 copy.21
  18.4 0.1 copy.22
  18.5 0.1 copy.19
  18.6 0.1 copy.20
  18.7 0.0 collective-permute-done
  18.7 0.6 gather_fusion.3
  19.3 0.1 compare_select_fusion
  19.3 2.3 multiply_convert_fusion
  21.6 0.6 fusion.5
  22.2 1.2 fusion.20
  23.4 0.0 reduce-scatter.3.cloned.1.call-update
  23.4 0.0 reduce-scatter.5.cloned.1.call-start
  23.5 0.1 copy.30
  23.5 0.1 copy.29
  23.6 0.1 copy.28
  23.7 0.1 copy.31
  23.8 0.1 copy.32
  23.8 2.3 fusion.3
  26.1 2.3 fusion.21
  28.4 0.0 reduce-scatter.5.cloned.1.call-update
  28.4 243.6 %reduce-scatter.3.cloned.1.call-done = f32[1,48,48]{2,1,0:T(8,128)} async-done(((f32[32,48,48]{2,1,0:T(8,128)}), f32[1,48,48]{2,1,0:T(8,128)}) %reduce-scatter.3.cloned.1.call-update) | async-done | bytes 9232 | tf_op jit(solution)/shard_map/reduce_scatter | solution.py:47
  272.1 0.8 select_add_fusion
  272.9 0.1 copy.27
  273.0 0.8 fusion.15
  273.8 4.4 custom-call.8
  278.2 0.6 compare_reduce_fusion
  278.8 0.7 select_select_fusion
  279.5 3.7 custom-call.9
  283.2 233.3 %reduce-scatter.5.cloned.1.call-done = f32[1,48,512]{2,1,0:T(8,128)} async-done(((f32[32,48,512]{2,1,0:T(8,128)}), f32[1,48,512]{2,1,0:T(8,128)}) %reduce-scatter.5.cloned.1.call-update) | async-done | bytes 98320 | tf_op jit(solution)/shard_map/reduce_scatter | solution.py:48
  516.4 1.8 multiply_reduce_fusion
  518.2 114.4 %psum.7 = f32[]{:T(128)} all-reduce(f32[]{:T(128)} %get-tuple-element.11), channel_id=1, replica_groups=mesh['stretch'=16,'worker'=32] {'worker'}, use_global_device_ids=true, to_apply=%region_5.6 | all-reduce | flops 1 | bytes 8 | tf_op jit(solution)/shard_map/psum | solution.py:53
  633.4 0.6 fusion.12
  (16 shorter events, 0.1 us)
Async XLA Ops:
  6.5 4.9 copy-start
  6.5 265.5 %reduce-scatter.3.cloned.1.call-start = ((), (), s32[]{:S(2)}) async-start(), calls=%async_computation.2 | async-start | bytes 811008 | tf_op jit(solution)/shard_map/reduce_scatter | solution.py:47
  7.4 11.3 %collective-permute-start = (f32[32,16]{1,0:T(8,128)S(1)}, f32[32,16]{1,0:T(8,128)S(1)}, u32[]{:S(2)}, u32[]{:S(2)}) collective-permute-start(f32[32,16]{1,0:T(8,128)S(1)} %bitcast.94), channel_id=1, source_target_pairs={{0,32},{32,64},{64,96},{96,128},{128,160},{160,192},{192,224},{224... | collective-permute-start | bytes 6152 | tf_op jit(solution)/shard_map/ppermute | solution.py:9
  13.3 3.2 copy-start.3
  13.3 4.0 copy-start.1
  17.2 4.5 copy-start.2
  23.4 493.0 %reduce-scatter.5.cloned.1.call-start = ((), (), s32[]{:S(2)}) async-start(), calls=%async_computation.3 | async-start | bytes 3244032 | tf_op jit(solution)/shard_map/reduce_scatter | solution.py:48
Sparse Core Ops, SparseCore 0:
  23.5 248.4 reduce-scatter.2
  275.1 241.2 reduce-scatter.4
where the time goes:
time: 641 us
  waiting for transfers between devices  477 us (74%)
  blocking collectives  114 us (18%)
  other arithmetic  20.2 us (3%)
  between operations  14.3 us (2%)
  local copies, waits for them, and re-layouts  7.22 us (1%)
    reduce_scatter x1, waiting for transfers between devices, body(): lax.psum_scatter(gram_part, 'worker', scatter_dimension=0, tiled=True)  244 us
    reduce_scatter x1, waiting for transfers between devices, body(): lax.psum_scatter(proj_part, 'worker', scatter_dimension=0, tiled=True)  233 us
    psum x1, blocking collectives, body(): total = lax.psum(jnp.sum(right * right), 'worker')  114 us
  transfers between devices with their start and end apart: 3, of which 2 were waited for; matrix products, arithmetic and copies ran while one was open for 4% of the time, Pallas kernels for 0%

commit v1 on v0

v1 whole, which is shorter than its diff:
```python
import functools

import jax
import jax.numpy as jnp
from jax import lax
from jax.experimental import pallas as pl
from jax.experimental.pallas import tpu as pltpu
from jax.sharding import PartitionSpec as P

NX = 4
NZ = 8
PAIRS = NZ // 2
NEAR = NX * 2
WORKERS = NX * NZ
NEAR_GROUPS = [[x * NZ + 2 * p + q for x in range(NX) for q in range(2)] for p in range(PAIRS)]
FAR_GROUPS = [[x * NZ + 2 * p + q for p in range(PAIRS)] for x in range(NX) for q in range(2)]
GRAM_LANES = 128
LOW_LANE = 64


def place():
    me = lax.axis_index("worker")
    column, depth = me // NZ, me % NZ
    return me, column, depth // 2, depth % 2


def arrange_kernel(order, theta, message):
    for d in range(NEAR):
        for j in range(PAIRS):
            owner = (d // 2) * NZ + 2 * j + d % 2
            message[d, j] = theta[order[owner]]


def contract_kernel(order, sizes, gates, rows_in, weights, sketch, out, block):
    _, column, pair, parity = place()
    near, _, _, depth, width = rows_in.shape
    rank = sketch.shape[1]
    total = near * depth
    lane = lax.broadcasted_iota(jnp.int32, (depth, weights.shape[2]), 1)
    sub = lax.broadcasted_iota(jnp.int32, (depth, 1), 0)
    bond = lax.broadcasted_iota(jnp.int32, (width, rank), 0)
    for j in range(PAIRS):
        blk = order[column * NZ + 2 * j + parity]
        size = sizes[blk]
        mix = [[gates[blk * 9 + g * 3 + p] for p in range(3)] for g in range(3)]
        for s in range(near):
            first = ((s // 2) * NZ + 2 * pair + s % 2) * depth
            scale = jnp.sum(jnp.where(lane == blk, weights[s], 0.0), axis=1, keepdims=True)
            scale = jnp.where(sub + first < size, scale, 0.0)
            x0, x1, x2 = (rows_in[s, j, p].astype(jnp.float32) for p in range(3))
            for g in range(3):
                mixed = (mix[g][0] * x0 + mix[g][1] * x1 + mix[g][2] * x2) * scale
                at = g * total + s * depth
                block[at : at + depth, :] = mixed.astype(jnp.bfloat16)
        live = jnp.where(bond < size, sketch[...].astype(jnp.float32), 0.0).astype(jnp.bfloat16)
        rows = block[...]
        sample = jnp.dot(rows, live, preferred_element_type=jnp.float32).astype(jnp.bfloat16)
        over_rows = (((0,), (0,)), ((), ()))
        projected = lax.dot_general(sample, rows, over_rows, preferred_element_type=jnp.float32)
        gram = lax.dot_general(sample, sample, over_rows, preferred_element_type=jnp.float32)
        high = gram.astype(jnp.bfloat16)
        low = (gram - high.astype(jnp.float32)).astype(jnp.bfloat16)
        out[j, :, :width] = projected.astype(jnp.bfloat16)
        out[j, :, width : width + rank] = high
        out[j, :, width + LOW_LANE : width + LOW_LANE + rank] = low


def solve_kernel(order, sizes, ranks, parts, right_out, norm_out, wide):
    me = place()[0]
    pairs, rank, full = parts.shape
    width = full - GRAM_LANES
    blk = order[me]
    size = sizes[blk]
    kept = jnp.minimum(ranks[blk], size // 2)

    tail = parts[0, :, width:].astype(jnp.float32)
    for p in range(1, pairs):
        tail = tail + parts[p, :, width:].astype(jnp.float32)
    row = lax.broadcasted_iota(jnp.int32, (rank, GRAM_LANES), 0)
    lane = lax.broadcasted_iota(jnp.int32, (rank, GRAM_LANES), 1)
    gram = tail + pltpu.roll(tail, GRAM_LANES - LOW_LANE, 1)
    gram = jnp.where((row < kept) & (lane < kept), gram, 0.0)
    gram = jnp.where((row == lane) & (row >= kept), 1.0, gram)
    work = jnp.where(lane == row + LOW_LANE, 1.0, gram)

    step = 8
    inverse = []
    for k0 in range(0, rank, step):
        height = rank - k0
        heads = [work[j : j + 1, :] for j in range(step)]
        cols = [
            jnp.broadcast_to(work[:, k0 + j : k0 + j + 1], (height, GRAM_LANES))
            for j in range(step)
        ]
        scaled = []
        for j in range(step):
            pivot = cols[j][j : j + 1, :]
            inv = 1.0 / pivot
            scaled.append(heads[j] * inv)
            inverse.append(heads[j] * lax.rsqrt(pivot))
            for i in range(j + 1, step):
                factor = cols[j][i : i + 1, :]
                heads[i] = heads[i] - factor * scaled[j]
                cols[i] = cols[i] - cols[j] * (factor * inv)
        if height > step:
            work = work[step:, :]
            for j in range(step):
                work = work - cols[j][step:, :] * scaled[j]
    lower_inverse = jnp.concatenate(inverse, axis=0)
    lower_inverse = jnp.where(lane >= LOW_LANE, lower_inverse, 0.0)

    projected = parts[0, :, :width].astype(jnp.float32)
    for p in range(1, pairs):
        projected = projected + parts[p, :, :width].astype(jnp.float32)
    prow = lax.broadcasted_iota(jnp.int32, (rank, width), 0)
    plane = lax.broadcasted_iota(jnp.int32, (rank, width), 1)
    wide[...] = jnp.zeros_like(wide)
    wide[LOW_LANE : LOW_LANE + rank, :] = jnp.where((prow < kept) & (plane < size), projected, 0.0)
    right = jnp.dot(
        lower_inverse,
        wide[...],
        preferred_element_type=jnp.float32,
        precision=lax.Precision.HIGHEST,
    )
    right_out[...] = right
    square = right * right
    folded = square[:, 0:128]
    for c in range(128, width, 128):
        folded = folded + square[:, c : c + 128]
    folded = jnp.sum(folded, axis=0, keepdims=True)
    norm_out[...] = jnp.broadcast_to(folded, norm_out.shape)


def finish_kernel(count, right, norms, out):
    total = jnp.sum(jnp.sum(norms[...], axis=0, keepdims=True), axis=1, keepdims=True)
    out[...] = (right[...] * jnp.sqrt(count / total)).astype(out.dtype)


SMEM = pl.BlockSpec(memory_space=pltpu.SMEM)
VMEM = pl.BlockSpec(memory_space=pltpu.VMEM)


def body(theta, gates, edge_weights, sizes, ranks, order, sketch):
    theta, gates, edge_weights, sketch = theta[0], gates[0], edge_weights[0], sketch[0]
    sizes, ranks, order = sizes[0], ranks[0], order[0]
    count, phys, depth, width = theta.shape
    rank = sketch.shape[1]
    stretches = lax.axis_size("stretch")
    left = lax.ppermute(
        edge_weights, "stretch", [(i, (i + 1) % stretches) for i in range(stretches)]
    )
    message = pl.pallas_call(
        arrange_kernel,
        out_shape=jax.ShapeDtypeStruct((NEAR, PAIRS, phys, depth, width), theta.dtype),
        in_specs=[SMEM, VMEM],
        out_specs=VMEM,
        name="arrange",
    )(order, theta)
    rows_in = lax.all_to_all(
        message, "worker", 0, 0, tiled=True, axis_index_groups=NEAR_GROUPS
    )
    weights = lax.all_to_all(
        jnp.broadcast_to(left.T[None], (NEAR, depth, count)),
        "worker",
        0,
        0,
        tiled=True,
        axis_index_groups=NEAR_GROUPS,
    )
    parts = pl.pallas_call(
        contract_kernel,
        out_shape=jax.ShapeDtypeStruct((PAIRS, rank, width + GRAM_LANES), jnp.bfloat16),
        in_specs=[SMEM, SMEM, SMEM, VMEM, VMEM, VMEM],
        out_specs=VMEM,
        scratch_shapes=[pltpu.VMEM((3 * NEAR * depth, width), jnp.bfloat16)],
        compiler_params=pltpu.CompilerParams(vmem_limit_bytes=32 * 2**20),
        name="contract",
    )(order, sizes, gates.reshape(-1), rows_in, weights, sketch)
    parts = lax.all_to_all(parts, "worker", 0, 0, tiled=True, axis_index_groups=FAR_GROUPS)
    right, norms = pl.pallas_call(
        solve_kernel,
        out_shape=(
            jax.ShapeDtypeStruct((rank, width), jnp.float32),
            jax.ShapeDtypeStruct((WORKERS, 128), jnp.float32),
        ),
        in_specs=[SMEM, SMEM, SMEM, VMEM],
        out_specs=(VMEM, VMEM),
        scratch_shapes=[pltpu.VMEM((GRAM_LANES, width), jnp.float32)],
        name="solve",
    )(order, sizes, ranks, parts)
    norms = lax.all_to_all(norms, "worker", 0, 0, tiled=True)
    factors = pl.pallas_call(
        functools.partial(finish_kernel, float(count)),
        out_shape=jax.ShapeDtypeStruct((rank, width), jnp.bfloat16),
        in_specs=[VMEM, VMEM],
        out_specs=VMEM,
        name="finish",
    )(right, norms)
    return factors[None, None]


def solution(mesh):
    return jax.shard_map(
        body,
        mesh=mesh,
        in_specs=(
            P("stretch", None, None, "worker", None),
            P("stretch", None, None, None),
            P("stretch", None, "worker"),
            P("stretch", None),
            P("stretch", None),
            P("stretch", None),
            P("stretch", None, None),
        ),
        out_specs=P("stretch", "worker", None, None),
        check_vma=False,
    )
```

time: 641 us -> 98 us (0.15)
  the two profiles are of different devices: /device:TPU:8 before, /device:TPU:2 now
where the time goes in v1:
time: 98 us; the launch traced here: 97.6 us
  blocking collectives  41.3 us (42%)
  waiting for transfers between devices  31.9 us (33%)
  starting transfers between devices  11.9 us (12%)
  Pallas kernels  10 us (10%)
  local copies, waits for them, and re-layouts  1.73 us (2%)
    all_to_all x1, blocking collectives, body(): lax.all_to_all(parts, 'worker', 0, 0, tiled=True, axis_index_groups=FAR_G...  22.6 us
    all_to_all x1, blocking collectives, body(): norms = lax.all_to_all(norms, 'worker', 0, 0, tiled=True)  18.7 us
    ppermute x1, waiting for transfers between devices, body(): lax.ppermute(edge_weights, 'stretch', [(i, (i + 1) % stretches) for i in...  17.2 us
    all_to_all x1, waiting for transfers between devices, body(): lax.all_to_all(message, 'worker', 0, 0, tiled=True, axis_index_groups=NEA...  10.9 us
    all_to_all x1, starting transfers between devices, body(): lax.all_to_all(jnp.broadcast_to(left.T[None], (NEAR, depth, count)), 'wor...  6.01 us
    all_to_all x1, starting transfers between devices, body(): lax.all_to_all(message, 'worker', 0, 0, tiled=True, axis_index_groups=NEA...  3.98 us
    all_to_all x1, waiting for transfers between devices, body(): lax.all_to_all(jnp.broadcast_to(left.T[None], (NEAR, depth, count)), 'wor...  3.86 us
    pallas_call x1, Pallas kernels, body(): pl.pallas_call(solve_kernel, out_shape=(jax.ShapeDtypeStruct((rank, width...  2.98 us
  transfers between devices with their start and end apart: 3, of which 3 were waited for; matrix products, arithmetic and copies ran while one was open for 2% of the time, Pallas kernels for 3%

profile of v1, /device:TPU:2, one launch (start us, length us, event | category | flops | bytes accessed | tf_op | source)
XLA Modules:
  0.0 97.6 jit_solution(15651707722542810855)
XLA Ops:
  0.0 1.9 %collective-permute-start = (f32[32,16]{0,1:T(8,128)}, f32[32,16]{0,1:T(8,128)S(1)}, u32[]{:S(2)}, u32[]{:S(2)}) collective-permute-start(f32[32,16]{0,1:T(8,128)} %bitcast.23), channel_id=1, source_target_pairs={{0,32},{32,64},{64,96},{96,128},{128,160},{160,192},{192,224},{224... | collective-permute-start | bytes 6152 | tf_op jit(solution)/shard_map/ppermute | solution.py:149
  1.9 17.2 %collective-permute-done = f32[32,16]{0,1:T(8,128)S(1)} collective-permute-done((f32[32,16]{0,1:T(8,128)}, f32[32,16]{0,1:T(8,128)S(1)}, u32[]{:S(2)}, u32[]{:S(2)}) %collective-permute-start) | collective-permute-done | bytes 2080 | tf_op jit(solution)/shard_map/ppermute | solution.py:149
  19.1 0.7 reshape.3
  19.8 6.0 %all-to-all-start.1 = ((f32[8,1,512]{2,1,0:T(1,128)}), f32[8,1,512]{2,1,0:T(1,128)S(1)}, u32[]{:S(2)}, u32[]{:S(2)}) async-start(f32[8,1,512]{2,1,0:T(1,128)} %reshape.3), calls=%async_computation.1 | async-start | bytes 32768 | tf_op jit(solution)/shard_map/all_to_all | solution.py:162
  25.9 2.7 %arrange.1 = bf16[8,4,3,16,512]{4,3,2,1,0:T(8,128)(2,1)} custom-call(s32[32]{0:T(128)} %bitcast.13, bf16[32,3,16,512]{3,2,1,0:T(8,128)(2,1)} %bitcast.18), custom_call_target="tpu_custom_call" | custom-call | tf_op jit(solution)/shard_map/arrange/pallas_call | solution.py:152
  28.5 0.0 copy-start.2
  28.5 0.0 copy-start.3
  28.5 0.0 copy-start
  28.5 0.0 copy-start.1
  28.5 3.9 %all-to-all-done.1 = f32[8,1,512]{2,1,0:T(1,128)S(1)} async-done(((f32[8,1,512]{2,1,0:T(1,128)}), f32[8,1,512]{2,1,0:T(1,128)S(1)}, u32[]{:S(2)}, u32[]{:S(2)}) %all-to-all-start.1) | async-done | bytes 16416 | tf_op jit(solution)/shard_map/all_to_all | solution.py:162
  32.4 4.0 %all-to-all-start = ((bf16[8,4,3,16,512]{4,3,2,1,0:T(8,128)(2,1)}), bf16[8,4,3,16,512]{4,3,2,1,0:T(8,128)(2,1)S(1)}, u32[]{:S(2)}, u32[]{:S(2)}) async-start(bf16[8,4,3,16,512]{4,3,2,1,0:T(8,128)(2,1)} %arrange.1), calls=%async_computation | async-start | bytes 3145728 | tf_op jit(solution)/shard_map/all_to_all | solution.py:159
  36.4 0.0 copy-done.2
  36.4 0.1 copy.12
  36.5 0.0 copy-done.3
  36.5 0.1 copy.11
  36.6 0.2 reshape_squeeze.3.gates
  36.8 0.5 broadcast.1
  37.3 0.7 reduce
  38.0 0.1 reshape.4.weights
  38.1 10.9 %all-to-all-done.rows_in = bf16[8,4,3,16,512]{4,3,2,1,0:T(8,128)(2,1)S(1)} async-done(((bf16[8,4,3,16,512]{4,3,2,1,0:T(8,128)(2,1)}), bf16[8,4,3,16,512]{4,3,2,1,0:T(8,128)(2,1)S(1)}, u32[]{:S(2)}, u32[]{:S(2)}) %all-to-all-start) | async-done | bytes 1572896 | tf_op jit(solution)/shard_map/all_to_all | solution.py:159
  49.0 0.0 copy-done
  49.0 0.0 copy-done.1
  49.0 2.7 %contract.1 = bf16[4,48,640]{2,1,0:T(8,128)(2,1)S(1)} custom-call(s32[32]{0:T(128)S(1)} %bitcast.15, s32[32]{0:T(128)S(1)} %bitcast.17, f32[288]{0:T(512)S(1)} %reshape_squeeze.3.gates, bf16[8,4,3,16,512]{4,3,2,1,0:T(8,128)(2,1)S(1)} %all-to-all-done.rows_in, f32[8,16,32]{2,1,0:T(8,128)S(1)} %reshape.4.weights, bf16[512,48]{1,0:T(8,128)(2,1)S(1)} %bitcast.12), custom_call_target="tpu_custom_call" | custom-call | tf_op jit(solution)/shard_map/contract/pallas_call | solution.py:170
  51.7 22.6 %all_to_all.26.parts = bf16[4,48,640]{2,1,0:T(8,128)(2,1)} all-to-all(bf16[4,48,640]{2,1,0:T(8,128)(2,1)S(1)} %contract.1), channel_id=1, replica_groups={{0,2,4,6},{1,3,5,7},{8,10,12,14},{9,11,13,15},{16,18,20,22},{17,19,21,2..., dimensions={0} | all-to-all | bytes 491520 | tf_op jit(solution)/shard_map/all_to_all | solution.py:179
  74.3 3.0 %solve.1 = (f32[48,512]{1,0:T(8,128)}, f32[32,128]{1,0:T(8,128)}) custom-call(s32[32]{0:T(128)} %bitcast.14, s32[32]{0:T(128)} %bitcast.16, s32[32]{0:T(128)} %bitcast.22, bf16[4,48,640]{2,1,0:T(8,128)(2,1)} %all_to_all.26.parts), custom_call_target="tpu_custom_call" | custom-call | tf_op jit(solution)/shard_map/solve/pallas_call | solution.py:180
  77.3 18.7 %all_to_all.27 = f32[32,1,128]{2,1,0:T(1,128)} all-to-all(f32[32,1,128]{2,1,0:T(1,128)} %bitcast.20), channel_id=1, replica_groups=mesh['stretch'=16,'worker'=32] {'worker'}, dimensions={0} | all-to-all | bytes 32768 | tf_op jit(solution)/shard_map/all_to_all | solution.py:191
  96.0 1.6 %finish.1 = bf16[48,512]{1,0:T(8,128)(2,1)} custom-call(f32[48,512]{1,0:T(8,128)} %get-tuple-element.7.right, f32[32,128]{1,0:T(8,128)} %bitcast.19), custom_call_target="tpu_custom_call" | custom-call | tf_op jit(solution)/shard_map/finish/pallas_call | solution.py:192
  (1 shorter events, 0.0 us)
Async XLA Ops:
  0.0 19.1 %collective-permute-start = (f32[32,16]{0,1:T(8,128)}, f32[32,16]{0,1:T(8,128)S(1)}, u32[]{:S(2)}, u32[]{:S(2)}) collective-permute-start(f32[32,16]{0,1:T(8,128)} %bitcast.23), channel_id=1, source_target_pairs={{0,32},{32,64},{64,96},{96,128},{128,160},{160,192},{192,224},{224... | collective-permute-start | bytes 6152 | tf_op jit(solution)/shard_map/ppermute | solution.py:149
  19.8 12.6 %all-to-all-start.1 = ((f32[8,1,512]{2,1,0:T(1,128)}), f32[8,1,512]{2,1,0:T(1,128)S(1)}, u32[]{:S(2)}, u32[]{:S(2)}) async-start(f32[8,1,512]{2,1,0:T(1,128)} %reshape.3), calls=%async_computation.1 | async-start | bytes 32768 | tf_op jit(solution)/shard_map/all_to_all | solution.py:162
  28.5 7.9 %copy-start.2 = (bf16[1,512,48]{1,2,0:T(8,128)(2,1)S(1)}, bf16[1,512,48]{1,2,0:T(8,128)(2,1)}, u32[]{:S(2)}) copy-start(bf16[1,512,48]{1,2,0:T(8,128)(2,1)} %param.13) | copy-start | bytes 147460
  28.5 8.0 %copy-start.3 = (f32[1,32,3,3]{1,0,3,2:T(1,128)S(1)}, f32[1,32,3,3]{1,0,3,2:T(1,128)}, u32[]{:S(2)}) copy-start(f32[1,32,3,3]{1,0,3,2:T(1,128)} %param.8) | copy-start | bytes 3460
  28.5 20.4 %copy-start = (s32[1,32]{1,0:T(1,128)S(1)}, s32[1,32]{1,0:T(1,128)}, u32[]{:S(2)}) copy-start(s32[1,32]{1,0:T(1,128)} %param.12) | copy-start | bytes 388
  28.5 20.4 %copy-start.1 = (s32[1,32]{1,0:T(1,128)S(1)}, s32[1,32]{1,0:T(1,128)}, u32[]{:S(2)}) copy-start(s32[1,32]{1,0:T(1,128)} %param.10) | copy-start | bytes 388
  32.4 16.6 %all-to-all-start = ((bf16[8,4,3,16,512]{4,3,2,1,0:T(8,128)(2,1)}), bf16[8,4,3,16,512]{4,3,2,1,0:T(8,128)(2,1)S(1)}, u32[]{:S(2)}, u32[]{:S(2)}) async-start(bf16[8,4,3,16,512]{4,3,2,1,0:T(8,128)(2,1)} %arrange.1), calls=%async_computation | async-start | bytes 3145728 | tf_op jit(solution)/shard_map/all_to_all | solution.py:159

commit v2 on v1

--- a/solution.py
+++ b/solution.py
@@ -24,38 +24,43 @@
     return me, column, depth // 2, depth % 2
 
 
-def arrange_kernel(order, theta, message):
+def mix_kernel(gates, theta, mixed):
+    for blk in range(theta.shape[0]):
+        x = [theta[blk, p].astype(jnp.float32) for p in range(3)]
+        for g in range(3):
+            mixed[blk, g] = (
+                gates[g, 0, blk] * x[0] + gates[g, 1, blk] * x[1] + gates[g, 2, blk] * x[2]
+            )
+
+
+def weigh_kernel(order, sizes, mixed, left, message):
+    depth, width = mixed.shape[2:]
+    first = place()[0] * depth
+    columns = left[...]
+    lane = lax.broadcasted_iota(jnp.int32, columns.shape, 1)
+    row = lax.broadcasted_iota(jnp.int32, (depth, 1), 0) + first
+    bond = lax.broadcasted_iota(jnp.int32, (1, width), 1)
     for d in range(NEAR):
         for j in range(PAIRS):
-            owner = (d // 2) * NZ + 2 * j + d % 2
-            message[d, j] = theta[order[owner]]
-
-
-def contract_kernel(order, sizes, gates, rows_in, weights, sketch, out, block):
-    _, column, pair, parity = place()
-    near, _, _, depth, width = rows_in.shape
-    rank = sketch.shape[1]
-    total = near * depth
-    lane = lax.broadcasted_iota(jnp.int32, (depth, weights.shape[2]), 1)
-    sub = lax.broadcasted_iota(jnp.int32, (depth, 1), 0)
-    bond = lax.broadcasted_iota(jnp.int32, (width, rank), 0)
-    for j in range(PAIRS):
-        blk = order[column * NZ + 2 * j + parity]
-        size = sizes[blk]
-        mix = [[gates[blk * 9 + g * 3 + p] for p in range(3)] for g in range(3)]
-        for s in range(near):
-            first = ((s // 2) * NZ + 2 * pair + s % 2) * depth
-            scale = jnp.sum(jnp.where(lane == blk, weights[s], 0.0), axis=1, keepdims=True)
-            scale = jnp.where(sub + first < size, scale, 0.0)
-            x0, x1, x2 = (rows_in[s, j, p].astype(jnp.float32) for p in range(3))
+            blk = order[(d // 2) * NZ + 2 * j + d % 2]
+            size = sizes[blk]
+            scale = jnp.sum(jnp.where(lane == blk, columns, 0.0), axis=1, keepdims=True)
+            scale = jnp.where(row < size, scale, 0.0)
             for g in range(3):
-                mixed = (mix[g][0] * x0 + mix[g][1] * x1 + mix[g][2] * x2) * scale
-                at = g * total + s * depth
-                block[at : at + depth, :] = mixed.astype(jnp.bfloat16)
-        live = jnp.where(bond < size, sketch[...].astype(jnp.float32), 0.0).astype(jnp.bfloat16)
-        rows = block[...]
-        sample = jnp.dot(rows, live, preferred_element_type=jnp.float32).astype(jnp.bfloat16)
-        over_rows = (((0,), (0,)), ((), ()))
+                rows = jnp.where(bond < size, mixed[blk, g] * scale, 0.0)
+                message[d, j, g] = rows.astype(jnp.bfloat16)
+
+
+def contract_kernel(rows_in, sketch, out):
+    near, pairs, phys, depth, width = rows_in.shape
+    rank = sketch.shape[0]
+    basis = sketch[...]
+    over_bond = (((1,), (1,)), ((), ()))
+    over_rows = (((0,), (0,)), ((), ()))
+    for j in range(pairs):
+        rows = rows_in[:, j].reshape(near * phys * depth, width)
+        sample = lax.dot_general(rows, basis, over_bond, preferred_element_type=jnp.float32)
+        sample = sample.astype(jnp.bfloat16)
         projected = lax.dot_general(sample, rows, over_rows, preferred_element_type=jnp.float32)
         gram = lax.dot_general(sample, sample, over_rows, preferred_element_type=jnp.float32)
         high = gram.astype(jnp.bfloat16)
@@ -113,9 +118,8 @@
     for p in range(1, pairs):
         projected = projected + parts[p, :, :width].astype(jnp.float32)
     prow = lax.broadcasted_iota(jnp.int32, (rank, width), 0)
-    plane = lax.broadcasted_iota(jnp.int32, (rank, width), 1)
     wide[...] = jnp.zeros_like(wide)
-    wide[LOW_LANE : LOW_LANE + rank, :] = jnp.where((prow < kept) & (plane < size), projected, 0.0)
+    wide[LOW_LANE : LOW_LANE + rank, :] = jnp.where(prow < kept, projected, 0.0)
     right = jnp.dot(
         lower_inverse,
         wide[...],
@@ -147,35 +151,38 @@
     rank = sketch.shape[1]
     stretches = lax.axis_size("stretch")
     left = lax.ppermute(
-        edge_weights, "stretch", [(i, (i + 1) % stretches) for i in range(stretches)]
-    )
+        edge_weights.T, "stretch", [(i, (i + 1) % stretches) for i in range(stretches)]
+    )
+    mixed = pl.pallas_call(
+        mix_kernel,
+        out_shape=jax.ShapeDtypeStruct(theta.shape, jnp.float32),
+        in_specs=[SMEM, VMEM],
+        out_specs=VMEM,
+        compiler_params=pltpu.CompilerParams(vmem_limit_bytes=16 * 2**20),
+        cost_estimate=pl.CostEstimate(
+            flops=15 * theta.size, bytes_accessed=6 * theta.size, transcendentals=0
+        ),
+        name="mix",
+    )(jnp.transpose(gates, (1, 2, 0)), theta)
     message = pl.pallas_call(
-        arrange_kernel,
+        weigh_kernel,
         out_shape=jax.ShapeDtypeStruct((NEAR, PAIRS, phys, depth, width), theta.dtype),
-        in_specs=[SMEM, VMEM],
-        out_specs=VMEM,
-        name="arrange",
-    )(order, theta)
+        in_specs=[SMEM, SMEM, VMEM, VMEM],
+        out_specs=VMEM,
+        compiler_params=pltpu.CompilerParams(vmem_limit_bytes=16 * 2**20),
+        name="weigh",
+    )(order, sizes, mixed, left)
     rows_in = lax.all_to_all(
         message, "worker", 0, 0, tiled=True, axis_index_groups=NEAR_GROUPS
-    )
-    weights = lax.all_to_all(
-        jnp.broadcast_to(left.T[None], (NEAR, depth, count)),
-        "worker",
-        0,
-        0,
-        tiled=True,
-        axis_index_groups=NEAR_GROUPS,
     )
     parts = pl.pallas_call(
         contract_kernel,
         out_shape=jax.ShapeDtypeStruct((PAIRS, rank, width + GRAM_LANES), jnp.bfloat16),
-        in_specs=[SMEM, SMEM, SMEM, VMEM, VMEM, VMEM],
-        out_specs=VMEM,
-        scratch_shapes=[pltpu.VMEM((3 * NEAR * depth, width), jnp.bfloat16)],
-        compiler_params=pltpu.CompilerParams(vmem_limit_bytes=32 * 2**20),
+        in_specs=[VMEM, VMEM],
+        out_specs=VMEM,
+        compiler_params=pltpu.CompilerParams(vmem_limit_bytes=16 * 2**20),
         name="contract",
-    )(order, sizes, gates.reshape(-1), rows_in, weights, sketch)
+    )(rows_in, sketch.T)
     parts = lax.all_to_all(parts, "worker", 0, 0, tiled=True, axis_index_groups=FAR_GROUPS)
     right, norms = pl.pallas_call(
         solve_kernel,
@@ -186,6 +193,7 @@
         in_specs=[SMEM, SMEM, SMEM, VMEM],
         out_specs=(VMEM, VMEM),
         scratch_shapes=[pltpu.VMEM((GRAM_LANES, width), jnp.float32)],
+        compiler_params=pltpu.CompilerParams(vmem_limit_bytes=16 * 2**20),
         name="solve",
     )(order, sizes, ranks, parts)
     norms = lax.all_to_all(norms, "worker", 0, 0, tiled=True)
@@ -194,6 +202,7 @@
         out_shape=jax.ShapeDtypeStruct((rank, width), jnp.bfloat16),
         in_specs=[VMEM, VMEM],
         out_specs=VMEM,
+        compiler_params=pltpu.CompilerParams(vmem_limit_bytes=16 * 2**20),
         name="finish",
     )(right, norms)
     return factors[None, None]

time: 98 us -> 84.9 us (0.87)
  the two profiles are of different devices: /device:TPU:2 before, /device:TPU:16 now
where the time goes in v2:
time: 84.9 us; the launch traced here: 84.6 us
  blocking collectives  73.6 us (87%)
  Pallas kernels  6.86 us (8%)
  local copies, waits for them, and re-layouts  2.12 us (2%)
  starting transfers between devices  1.91 us (2%)
    all_to_all x1, blocking collectives, body(): lax.all_to_all(message, 'worker', 0, 0, tiled=True, axis_index_groups=NEA...  28.4 us
    all_to_all x1, blocking collectives, body(): lax.all_to_all(parts, 'worker', 0, 0, tiled=True, axis_index_groups=FAR_G...  28 us
    all_to_all x1, blocking collectives, body(): norms = lax.all_to_all(norms, 'worker', 0, 0, tiled=True)  17.2 us
    unnamed x11, local copies, waits for them, and re-layouts  2.12 us
    pallas_call x1, Pallas kernels, body(): pl.pallas_call(contract_kernel, out_shape=jax.ShapeDtypeStruct((PAIRS, ra...  2 us
    pallas_call x1, Pallas kernels, body(): pl.pallas_call(solve_kernel, out_shape=(jax.ShapeDtypeStruct((rank, width...  1.94 us
    ppermute x1, starting transfers between devices, body(): lax.ppermute(edge_weights.T, 'stretch', [(i, (i + 1) % stretches) for i i...  1.91 us
  transfers between devices with their start and end apart: 1, of which 0 were waited for; matrix products, arithmetic and copies ran while one was open for 1% of the time, Pallas kernels for 2%

profile of v2, /device:TPU:16, one launch (start us, length us, event | category | flops | bytes accessed | tf_op | source)
XLA Modules:
  0.0 84.6 jit_solution(3995298914254225601)
XLA Ops:
  0.0 1.9 %collective-permute-start = (f32[16,32]{1,0:T(8,128)}, f32[16,32]{1,0:T(8,128)S(1)}, u32[]{:S(2)}, u32[]{:S(2)}) collective-permute-start(f32[16,32]{1,0:T(8,128)} %bitcast.30), channel_id=1, source_target_pairs={{0,32},{32,64},{64,96},{96,128},{128,160},{160,192},{192,224},{224... | collective-permute-start | bytes 6152 | tf_op jit(solution)/shard_map/ppermute | solution.py:153
  1.9 0.7 copy.11
  2.6 0.0 copy-start
  2.6 1.4 %copy-done = bf16[1,32,3,16,512]{4,3,2,1,0:T(8,128)(2,1)S(1)} copy-done((bf16[1,32,3,16,512]{4,3,2,1,0:T(8,128)(2,1)S(1)}, bf16[1,32,3,16,512]{4,3,2,1,0:T(8,128)(2,1)}, u32[]{:S(2)}) %copy-start) | copy-done | bytes 1572888
  4.0 0.0 copy-start.2
  4.0 0.0 copy-start.3
  4.0 1.3 %mix.1.mixed = f32[32,3,16,512]{3,2,1,0:T(8,128)S(1)} custom-call(f32[3,3,32]{2,1,0:T(4,128)S(1)} %bitcast.23, bf16[32,3,16,512]{3,2,1,0:T(8,128)(2,1)S(1)} %bitcast.20), custom_call_target="tpu_custom_call" | custom-call | flops 11796480 | bytes 4718592 | tf_op jit(solution)/shard_map/mix/pallas_call | solution.py:156
  5.3 0.0 collective-permute-done.left
  5.3 0.0 copy-done.2
  5.3 0.0 copy-done.3
  5.3 0.9 %weigh.1 = bf16[8,4,3,16,512]{4,3,2,1,0:T(8,128)(2,1)S(1)} custom-call(s32[32]{0:T(128)S(1)} %bitcast.25, s32[32]{0:T(128)S(1)} %bitcast.27, f32[32,3,16,512]{3,2,1,0:T(8,128)S(1)} %mix.1.mixed, f32[16,32]{1,0:T(8,128)S(1)} %collective-permute-done.left), custom_call_target="tpu_custom_call" | custom-call | tf_op jit(solution)/shard_map/weigh/pallas_call | solution.py:167
  6.3 0.0 copy-start.1
  6.3 28.4 %all_to_all.21.rows_in = bf16[8,4,3,16,512]{4,3,2,1,0:T(8,128)(2,1)S(1)} all-to-all(bf16[8,4,3,16,512]{4,3,2,1,0:T(8,128)(2,1)S(1)} %weigh.1), channel_id=1, replica_groups={{0,1,8,9,16,17,24,25},{2,3,10,11,18,19,26,27},{4,5,12,13,20,21,28,29},{..., dimensions={0} | all-to-all | bytes 3145728 | tf_op jit(solution)/shard_map/all_to_all | solution.py:175
  34.7 0.0 copy-start.4
  34.7 0.0 copy-done.1
  34.7 2.0 %contract.1 = bf16[4,48,640]{2,1,0:T(8,128)(2,1)S(1)} custom-call(bf16[8,4,3,16,512]{4,3,2,1,0:T(8,128)(2,1)S(1)} %all_to_all.21.rows_in, bf16[48,512]{1,0:T(8,128)(2,1)S(1)} %bitcast.22), custom_call_target="tpu_custom_call" | custom-call | tf_op jit(solution)/shard_map/contract/pallas_call | solution.py:178
  36.7 28.0 %all_to_all.22.parts = bf16[4,48,640]{2,1,0:T(8,128)(2,1)S(1)} all-to-all(bf16[4,48,640]{2,1,0:T(8,128)(2,1)S(1)} %contract.1), channel_id=1, replica_groups={{0,2,4,6},{1,3,5,7},{8,10,12,14},{9,11,13,15},{16,18,20,22},{17,19,21,2..., dimensions={0} | all-to-all | bytes 491520 | tf_op jit(solution)/shard_map/all_to_all | solution.py:186
  64.7 0.0 copy-done.4
  64.7 1.9 %solve.1 = (f32[48,512]{1,0:T(8,128)S(1)}, f32[32,128]{1,0:T(8,128)S(1)}) custom-call(s32[32]{0:T(128)S(1)} %bitcast.26, s32[32]{0:T(128)S(1)} %bitcast.28, s32[32]{0:T(128)S(1)} %bitcast.29, bf16[4,48,640]{2,1,0:T(8,128)(2,1)S(1)} %all_to_all.22.parts), custom_call_target="tpu_custom_call" | custom-call | tf_op jit(solution)/shard_map/solve/pallas_call | solution.py:187
  66.7 17.2 %all_to_all.23 = f32[32,1,128]{2,1,0:T(1,128)S(1)} all-to-all(f32[32,1,128]{2,1,0:T(1,128)S(1)} %bitcast.24), channel_id=1, replica_groups=mesh['stretch'=16,'worker'=32] {'worker'}, dimensions={0} | all-to-all | bytes 32768 | tf_op jit(solution)/shard_map/all_to_all | solution.py:199
  83.9 0.7 finish.1
Async XLA Ops:
  0.0 5.3 %collective-permute-start = (f32[16,32]{1,0:T(8,128)}, f32[16,32]{1,0:T(8,128)S(1)}, u32[]{:S(2)}, u32[]{:S(2)}) collective-permute-start(f32[16,32]{1,0:T(8,128)} %bitcast.30), channel_id=1, source_target_pairs={{0,32},{32,64},{64,96},{96,128},{128,160},{160,192},{192,224},{224... | collective-permute-start | bytes 6152 | tf_op jit(solution)/shard_map/ppermute | solution.py:153
  2.6 1.4 %copy-start = (bf16[1,32,3,16,512]{4,3,2,1,0:T(8,128)(2,1)S(1)}, bf16[1,32,3,16,512]{4,3,2,1,0:T(8,128)(2,1)}, u32[]{:S(2)}) copy-start(bf16[1,32,3,16,512]{4,3,2,1,0:T(8,128)(2,1)} %param.7) | copy-start | bytes 4718596
  4.0 1.3 %copy-start.2 = (s32[1,32]{1,0:T(1,128)S(1)}, s32[1,32]{1,0:T(1,128)}, u32[]{:S(2)}) copy-start(s32[1,32]{1,0:T(1,128)} %param.12) | copy-start | bytes 388
  4.0 1.3 %copy-start.3 = (s32[1,32]{1,0:T(1,128)S(1)}, s32[1,32]{1,0:T(1,128)}, u32[]{:S(2)}) copy-start(s32[1,32]{1,0:T(1,128)} %param.10) | copy-start | bytes 388
  6.3 28.4 %copy-start.1 = (bf16[1,512,48]{1,2,0:T(8,128)(2,1)S(1)}, bf16[1,512,48]{1,2,0:T(8,128)(2,1)}, u32[]{:S(2)}) copy-start(bf16[1,512,48]{1,2,0:T(8,128)(2,1)} %param.13) | copy-start | bytes 147460
  34.7 30.0 %copy-start.4 = (s32[1,32]{1,0:T(1,128)S(1)}, s32[1,32]{1,0:T(1,128)}, u32[]{:S(2)}) copy-start(s32[1,32]{1,0:T(1,128)} %param.11) | copy-start | bytes 388

commit v3 on v2

--- a/solution.py
+++ b/solution.py
@@ -29,7 +29,9 @@
         x = [theta[blk, p].astype(jnp.float32) for p in range(3)]
         for g in range(3):
             mixed[blk, g] = (
-                gates[g, 0, blk] * x[0] + gates[g, 1, blk] * x[1] + gates[g, 2, blk] * x[2]
+                gates[g, 0, 0, blk] * x[0]
+                + gates[g, 1, 0, blk] * x[1]
+                + gates[g, 2, 0, blk] * x[2]
             )
 
 
@@ -51,40 +53,65 @@
                 message[d, j, g] = rows.astype(jnp.bfloat16)
 
 
-def contract_kernel(rows_in, sketch, out):
+def contract_kernel(rows_in, sketch, out, own):
     near, pairs, phys, depth, width = rows_in.shape
     rank = sketch.shape[0]
+    pair = place()[2]
     basis = sketch[...]
-    over_bond = (((1,), (1,)), ((), ()))
-    over_rows = (((0,), (0,)), ((), ()))
+    over_lanes = (((1,), (1,)), ((), ()))
+
+    def rows_of(j):
+        return rows_in[:, j].reshape(near * phys * depth, width)
+
+    samples = []
     for j in range(pairs):
-        rows = rows_in[:, j].reshape(near * phys * depth, width)
-        sample = lax.dot_general(rows, basis, over_bond, preferred_element_type=jnp.float32)
-        sample = sample.astype(jnp.bfloat16)
-        projected = lax.dot_general(sample, rows, over_rows, preferred_element_type=jnp.float32)
-        gram = lax.dot_general(sample, sample, over_rows, preferred_element_type=jnp.float32)
-        high = gram.astype(jnp.bfloat16)
-        low = (gram - high.astype(jnp.float32)).astype(jnp.bfloat16)
-        out[j, :, :width] = projected.astype(jnp.bfloat16)
-        out[j, :, width : width + rank] = high
-        out[j, :, width + LOW_LANE : width + LOW_LANE + rank] = low
-
-
-def solve_kernel(order, sizes, ranks, parts, right_out, norm_out, wide):
-    me = place()[0]
-    pairs, rank, full = parts.shape
-    width = full - GRAM_LANES
+        sample = lax.dot_general(
+            basis, rows_of(j), over_lanes, preferred_element_type=jnp.float32
+        )
+        samples.append(sample.astype(jnp.bfloat16))
+    for j in range(pairs):
+        sample = samples[j]
+        projected = jnp.dot(sample, rows_of(j), preferred_element_type=jnp.float32)
+        out[j] = projected.astype(jnp.bfloat16)
+
+        @pl.when(pair == j)
+        def _():
+            own[...] = projected
+
+
+def solve_kernel(order, sizes, ranks, parts, own, sketch, right_out, norm_out, wide):
+    me, _, pair, _ = place()
+    pairs, rank, width = parts.shape
     blk = order[me]
     size = sizes[blk]
     kept = jnp.minimum(ranks[blk], size // 2)
 
-    tail = parts[0, :, width:].astype(jnp.float32)
-    for p in range(1, pairs):
-        tail = tail + parts[p, :, width:].astype(jnp.float32)
+    projected = own[...]
+    for p in range(pairs):
+        projected = projected + jnp.where(pair == p, 0.0, parts[p].astype(jnp.float32))
+    prow = lax.broadcasted_iota(jnp.int32, (rank, width), 0)
+    projected = jnp.where(prow < kept, projected, 0.0)
+    basis = jnp.concatenate(
+        [sketch[...].astype(jnp.float32), jnp.zeros((GRAM_LANES - rank, width), jnp.float32)], axis=0
+    )
+    over_lanes = (((1,), (1,)), ((), ()))
+    gram = lax.dot_general(
+        projected,
+        basis,
+        over_lanes,
+        preferred_element_type=jnp.float32,
+        precision=lax.Precision.HIGHEST,
+    )
+    mirror = lax.dot_general(
+        basis[:rank],
+        jnp.concatenate([projected, jnp.zeros((GRAM_LANES - rank, width), jnp.float32)], axis=0),
+        over_lanes,
+        preferred_element_type=jnp.float32,
+        precision=lax.Precision.HIGHEST,
+    )
     row = lax.broadcasted_iota(jnp.int32, (rank, GRAM_LANES), 0)
     lane = lax.broadcasted_iota(jnp.int32, (rank, GRAM_LANES), 1)
-    gram = tail + pltpu.roll(tail, GRAM_LANES - LOW_LANE, 1)
-    gram = jnp.where((row < kept) & (lane < kept), gram, 0.0)
+    gram = jnp.where((row < kept) & (lane < kept), 0.5 * (gram + mirror), 0.0)
     gram = jnp.where((row == lane) & (row >= kept), 1.0, gram)
     work = jnp.where(lane == row + LOW_LANE, 1.0, gram)
 
@@ -114,12 +141,8 @@
     lower_inverse = jnp.concatenate(inverse, axis=0)
     lower_inverse = jnp.where(lane >= LOW_LANE, lower_inverse, 0.0)
 
-    projected = parts[0, :, :width].astype(jnp.float32)
-    for p in range(1, pairs):
-        projected = projected + parts[p, :, :width].astype(jnp.float32)
-    prow = lax.broadcasted_iota(jnp.int32, (rank, width), 0)
     wide[...] = jnp.zeros_like(wide)
-    wide[LOW_LANE : LOW_LANE + rank, :] = jnp.where(prow < kept, projected, 0.0)
+    wide[LOW_LANE : LOW_LANE + rank, :] = projected
     right = jnp.dot(
         lower_inverse,
         wide[...],
@@ -163,7 +186,7 @@
             flops=15 * theta.size, bytes_accessed=6 * theta.size, transcendentals=0
         ),
         name="mix",
-    )(jnp.transpose(gates, (1, 2, 0)), theta)
+    )(jnp.transpose(gates, (1, 2, 0))[:, :, None], theta)
     message = pl.pallas_call(
         weigh_kernel,
         out_shape=jax.ShapeDtypeStruct((NEAR, PAIRS, phys, depth, width), theta.dtype),
@@ -175,11 +198,14 @@
     rows_in = lax.all_to_all(
         message, "worker", 0, 0, tiled=True, axis_index_groups=NEAR_GROUPS
     )
-    parts = pl.pallas_call(
+    parts, own = pl.pallas_call(
         contract_kernel,
-        out_shape=jax.ShapeDtypeStruct((PAIRS, rank, width + GRAM_LANES), jnp.bfloat16),
+        out_shape=(
+            jax.ShapeDtypeStruct((PAIRS, rank, width), jnp.bfloat16),
+            jax.ShapeDtypeStruct((rank, width), jnp.float32),
+        ),
         in_specs=[VMEM, VMEM],
-        out_specs=VMEM,
+        out_specs=(VMEM, VMEM),
         compiler_params=pltpu.CompilerParams(vmem_limit_bytes=16 * 2**20),
         name="contract",
     )(rows_in, sketch.T)
@@ -190,12 +216,12 @@
             jax.ShapeDtypeStruct((rank, width), jnp.float32),
             jax.ShapeDtypeStruct((WORKERS, 128), jnp.float32),
         ),
-        in_specs=[SMEM, SMEM, SMEM, VMEM],
+        in_specs=[SMEM, SMEM, SMEM, VMEM, VMEM, VMEM],
         out_specs=(VMEM, VMEM),
         scratch_shapes=[pltpu.VMEM((GRAM_LANES, width), jnp.float32)],
         compiler_params=pltpu.CompilerParams(vmem_limit_bytes=16 * 2**20),
         name="solve",
-    )(order, sizes, ranks, parts)
+    )(order, sizes, ranks, parts, own, sketch.T)
     norms = lax.all_to_all(norms, "worker", 0, 0, tiled=True)
     factors = pl.pallas_call(
         functools.partial(finish_kernel, float(count)),

time: 84.9 us -> 82.4 us (0.971)
  blocking collectives: 73.6 us -> 71.5 us
    all_to_all x1, blocking collectives: 28 us -> 25.9 us  [body(): lax.all_to_all(parts, 'worker', 0, 0, tiled=True, axis_index_groups=FAR_G...]
where the time goes in v3:
time: 82.4 us; the launch traced here: 82.1 us
  blocking collectives  71.5 us (87%)
  Pallas kernels  6.4 us (8%)
  local copies, waits for them, and re-layouts  2.13 us (3%)
  starting transfers between devices  1.91 us (2%)
    all_to_all x1, blocking collectives, body(): lax.all_to_all(message, 'worker', 0, 0, tiled=True, axis_index_groups=NEA...  28.4 us
    all_to_all x1, blocking collectives, body(): lax.all_to_all(parts, 'worker', 0, 0, tiled=True, axis_index_groups=FAR_G...  25.9 us
    all_to_all x1, blocking collectives, body(): norms = lax.all_to_all(norms, 'worker', 0, 0, tiled=True)  17.2 us
    pallas_call x1, Pallas kernels, body(): pl.pallas_call(solve_kernel, out_shape=(jax.ShapeDtypeStruct((rank, width...  2.33 us
    unnamed x11, local copies, waits for them, and re-layouts  2.12 us
    ppermute x1, starting transfers between devices, body(): lax.ppermute(edge_weights.T, 'stretch', [(i, (i + 1) % stretches) for i i...  1.91 us
  transfers between devices with their start and end apart: 1, of which 0 were waited for; matrix products, arithmetic and copies ran while one was open for 1% of the time, Pallas kernels for 2%

profile of v3, /device:TPU:16, one launch (start us, length us, event | category | flops | bytes accessed | tf_op | source)
XLA Modules:
  0.0 82.1 jit_solution(2965578554589097251)
XLA Ops:
  0.0 1.9 %collective-permute-start = (f32[16,32]{1,0:T(8,128)}, f32[16,32]{1,0:T(8,128)S(1)}, u32[]{:S(2)}, u32[]{:S(2)}) collective-permute-start(f32[16,32]{1,0:T(8,128)} %bitcast.31), channel_id=1, source_target_pairs={{0,32},{32,64},{64,96},{96,128},{128,160},{160,192},{192,224},{224... | collective-permute-start | bytes 6152 | tf_op jit(solution)/shard_map/ppermute | solution.py:176
  1.9 0.7 copy.11
  2.6 0.0 copy-start
  2.6 1.4 %copy-done = bf16[1,32,3,16,512]{4,3,2,1,0:T(8,128)(2,1)S(1)} copy-done((bf16[1,32,3,16,512]{4,3,2,1,0:T(8,128)(2,1)S(1)}, bf16[1,32,3,16,512]{4,3,2,1,0:T(8,128)(2,1)}, u32[]{:S(2)}) %copy-start) | copy-done | bytes 1572888
  4.0 0.0 copy-start.2
  4.0 0.0 copy-start.3
  4.0 1.3 %mix.1.mixed = f32[32,3,16,512]{3,2,1,0:T(8,128)S(1)} custom-call(f32[3,3,1,32]{3,2,1,0:T(1,128)S(1)} %broadcast_in_dim.6.gates, bf16[32,3,16,512]{3,2,1,0:T(8,128)(2,1)S(1)} %bitcast.20), custom_call_target="tpu_custom_call" | custom-call | flops 11796480 | bytes 4718592 | tf_op jit(solution)/shard_map/mix/pallas_call | solution.py:179
  5.3 0.0 collective-permute-done.left
  5.3 0.0 copy-done.2
  5.3 0.0 copy-done.3
  5.3 0.9 %weigh.1 = bf16[8,4,3,16,512]{4,3,2,1,0:T(8,128)(2,1)S(1)} custom-call(s32[32]{0:T(128)S(1)} %bitcast.25, s32[32]{0:T(128)S(1)} %bitcast.27, f32[32,3,16,512]{3,2,1,0:T(8,128)S(1)} %mix.1.mixed, f32[16,32]{1,0:T(8,128)S(1)} %collective-permute-done.left), custom_call_target="tpu_custom_call" | custom-call | tf_op jit(solution)/shard_map/weigh/pallas_call | solution.py:190
  6.2 0.0 copy-start.1
  6.3 28.4 %all_to_all.21.rows_in = bf16[8,4,3,16,512]{4,3,2,1,0:T(8,128)(2,1)S(1)} all-to-all(bf16[8,4,3,16,512]{4,3,2,1,0:T(8,128)(2,1)S(1)} %weigh.1), channel_id=1, replica_groups={{0,1,8,9,16,17,24,25},{2,3,10,11,18,19,26,27},{4,5,12,13,20,21,28,29},{..., dimensions={0} | all-to-all | bytes 3145728 | tf_op jit(solution)/shard_map/all_to_all | solution.py:198
  34.7 0.0 copy-start.4
  34.7 0.0 copy-done.1
  34.7 1.2 %contract.1 = (bf16[4,48,512]{2,1,0:T(8,128)(2,1)S(1)}, f32[48,512]{1,0:T(8,128)S(1)}) custom-call(bf16[8,4,3,16,512]{4,3,2,1,0:T(8,128)(2,1)S(1)} %all_to_all.21.rows_in, bf16[48,512]{1,0:T(8,128)(2,1)S(1)} %bitcast.21), custom_call_target="tpu_custom_call" | custom-call | tf_op jit(solution)/shard_map/contract/pallas_call | solution.py:201
  35.9 25.9 %all_to_all.22.parts = bf16[4,48,512]{2,1,0:T(8,128)(2,1)S(1)} all-to-all(bf16[4,48,512]{2,1,0:T(8,128)(2,1)S(1)} %get-tuple-element.9), channel_id=1, replica_groups={{0,2,4,6},{1,3,5,7},{8,10,12,14},{9,11,13,15},{16,18,20,22},{17,19,21,2..., dimensions={0} | all-to-all | bytes 393216 | tf_op jit(solution)/shard_map/all_to_all | solution.py:212
  61.8 0.0 copy-done.4
  61.8 2.3 %solve.1 = (f32[48,512]{1,0:T(8,128)S(1)}, f32[32,128]{1,0:T(8,128)S(1)}) custom-call(s32[32]{0:T(128)S(1)} %bitcast.26, s32[32]{0:T(128)S(1)} %bitcast.28, s32[32]{0:T(128)S(1)} %bitcast.29, bf16[4,48,512]{2,1,0:T(8,128)(2,1)S(1)} %all_to_all.22.parts, f32[48,512]{1,0:T(8,128)S(1)} %get-tuple-element.10.own, bf16[48,512]{1,0:T(8,128)(2,1)S(1)} %bitcast.22), custom_call_target="tpu_custom_call" | custom-call | tf_op jit(solution)/shard_map/solve/pallas_call | solution.py:213
  64.1 17.2 %all_to_all.23 = f32[32,1,128]{2,1,0:T(1,128)S(1)} all-to-all(f32[32,1,128]{2,1,0:T(1,128)S(1)} %bitcast.24), channel_id=1, replica_groups=mesh['stretch'=16,'worker'=32] {'worker'}, dimensions={0} | all-to-all | bytes 32768 | tf_op jit(solution)/shard_map/all_to_all | solution.py:225
  81.3 0.7 finish.1
  (1 shorter events, 0.0 us)
Async XLA Ops:
  0.0 5.3 %collective-permute-start = (f32[16,32]{1,0:T(8,128)}, f32[16,32]{1,0:T(8,128)S(1)}, u32[]{:S(2)}, u32[]{:S(2)}) collective-permute-start(f32[16,32]{1,0:T(8,128)} %bitcast.31), channel_id=1, source_target_pairs={{0,32},{32,64},{64,96},{96,128},{128,160},{160,192},{192,224},{224... | collective-permute-start | bytes 6152 | tf_op jit(solution)/shard_map/ppermute | solution.py:176
  2.6 1.4 %copy-start = (bf16[1,32,3,16,512]{4,3,2,1,0:T(8,128)(2,1)S(1)}, bf16[1,32,3,16,512]{4,3,2,1,0:T(8,128)(2,1)}, u32[]{:S(2)}) copy-start(bf16[1,32,3,16,512]{4,3,2,1,0:T(8,128)(2,1)} %param.7) | copy-start | bytes 4718596
  4.0 1.3 %copy-start.2 = (s32[1,32]{1,0:T(1,128)S(1)}, s32[1,32]{1,0:T(1,128)}, u32[]{:S(2)}) copy-start(s32[1,32]{1,0:T(1,128)} %param.12) | copy-start | bytes 388
  4.0 1.3 %copy-start.3 = (s32[1,32]{1,0:T(1,128)S(1)}, s32[1,32]{1,0:T(1,128)}, u32[]{:S(2)}) copy-start(s32[1,32]{1,0:T(1,128)} %param.10) | copy-start | bytes 388
  6.2 28.4 %copy-start.1 = (bf16[1,512,48]{1,2,0:T(8,128)(2,1)S(1)}, bf16[1,512,48]{1,2,0:T(8,128)(2,1)}, u32[]{:S(2)}) copy-start(bf16[1,512,48]{1,2,0:T(8,128)(2,1)} %param.13) | copy-start | bytes 147460
  34.7 27.1 %copy-start.4 = (s32[1,32]{1,0:T(1,128)S(1)}, s32[1,32]{1,0:T(1,128)}, u32[]{:S(2)}) copy-start(s32[1,32]{1,0:T(1,128)} %param.11) | copy-start | bytes 388

commit v4 on v3

--- a/solution.py
+++ b/solution.py
@@ -14,8 +14,9 @@
 WORKERS = NX * NZ
 NEAR_GROUPS = [[x * NZ + 2 * p + q for x in range(NX) for q in range(2)] for p in range(PAIRS)]
 FAR_GROUPS = [[x * NZ + 2 * p + q for p in range(PAIRS)] for x in range(NX) for q in range(2)]
-GRAM_LANES = 128
-LOW_LANE = 64
+LANES = 128
+HALF = 64
+OVER_LANES = (((1,), (1,)), ((), ()))
 
 
 def place():
@@ -53,76 +54,70 @@
                 message[d, j, g] = rows.astype(jnp.bfloat16)
 
 
-def contract_kernel(rows_in, sketch, out, own):
+def contract_kernel(rows_in, sketch, out, exact):
     near, pairs, phys, depth, width = rows_in.shape
-    rank = sketch.shape[0]
-    pair = place()[2]
     basis = sketch[...]
-    over_lanes = (((1,), (1,)), ((), ()))
 
     def rows_of(j):
         return rows_in[:, j].reshape(near * phys * depth, width)
 
-    samples = []
+    samples = [
+        lax.dot_general(basis, rows_of(j), OVER_LANES, preferred_element_type=jnp.float32)
+        for j in range(pairs)
+    ]
     for j in range(pairs):
-        sample = lax.dot_general(
-            basis, rows_of(j), over_lanes, preferred_element_type=jnp.float32
+        projected = jnp.dot(
+            samples[j].astype(jnp.bfloat16), rows_of(j), preferred_element_type=jnp.float32
         )
-        samples.append(sample.astype(jnp.bfloat16))
-    for j in range(pairs):
-        sample = samples[j]
-        projected = jnp.dot(sample, rows_of(j), preferred_element_type=jnp.float32)
         out[j] = projected.astype(jnp.bfloat16)
-
-        @pl.when(pair == j)
-        def _():
-            own[...] = projected
-
-
-def solve_kernel(order, sizes, ranks, parts, own, sketch, right_out, norm_out, wide):
+        exact[j] = projected
+
+
+def solve_kernel(order, sizes, ranks, parts, exact, sketch, right_out, norm_out):
     me, _, pair, _ = place()
     pairs, rank, width = parts.shape
     blk = order[me]
-    size = sizes[blk]
-    kept = jnp.minimum(ranks[blk], size // 2)
-
-    projected = own[...]
+    kept = jnp.minimum(ranks[blk], sizes[blk] // 2)
+
+    projected = exact[pair]
     for p in range(pairs):
         projected = projected + jnp.where(pair == p, 0.0, parts[p].astype(jnp.float32))
     prow = lax.broadcasted_iota(jnp.int32, (rank, width), 0)
     projected = jnp.where(prow < kept, projected, 0.0)
-    basis = jnp.concatenate(
-        [sketch[...].astype(jnp.float32), jnp.zeros((GRAM_LANES - rank, width), jnp.float32)], axis=0
-    )
-    over_lanes = (((1,), (1,)), ((), ()))
-    gram = lax.dot_general(
-        projected,
+    high = projected.astype(jnp.bfloat16)
+    rest = projected - high.astype(jnp.float32)
+    middle = rest.astype(jnp.bfloat16)
+    low = (rest - middle.astype(jnp.float32)).astype(jnp.bfloat16)
+
+    basis = sketch[...]
+    fill = jnp.zeros((LANES - rank, width), jnp.bfloat16)
+    three = lax.dot_general(
+        jnp.concatenate([high, middle, low], axis=0),
+        jnp.concatenate([basis, fill], axis=0),
+        OVER_LANES,
+        preferred_element_type=jnp.float32,
+    )
+    mirror = lax.dot_general(
         basis,
-        over_lanes,
+        jnp.concatenate([high, fill, middle, fill, low, fill], axis=0),
+        OVER_LANES,
         preferred_element_type=jnp.float32,
-        precision=lax.Precision.HIGHEST,
-    )
-    mirror = lax.dot_general(
-        basis[:rank],
-        jnp.concatenate([projected, jnp.zeros((GRAM_LANES - rank, width), jnp.float32)], axis=0),
-        over_lanes,
-        preferred_element_type=jnp.float32,
-        precision=lax.Precision.HIGHEST,
-    )
-    row = lax.broadcasted_iota(jnp.int32, (rank, GRAM_LANES), 0)
-    lane = lax.broadcasted_iota(jnp.int32, (rank, GRAM_LANES), 1)
+    )
+    gram = three[:rank] + three[rank : 2 * rank] + three[2 * rank :]
+    mirror = mirror[:, :LANES] + mirror[:, LANES : 2 * LANES] + mirror[:, 2 * LANES :]
+    row = lax.broadcasted_iota(jnp.int32, (rank, LANES), 0)
+    lane = lax.broadcasted_iota(jnp.int32, (rank, LANES), 1)
     gram = jnp.where((row < kept) & (lane < kept), 0.5 * (gram + mirror), 0.0)
     gram = jnp.where((row == lane) & (row >= kept), 1.0, gram)
-    work = jnp.where(lane == row + LOW_LANE, 1.0, gram)
-
-    step = 8
+    work = jnp.where(lane == row + HALF, 1.0, gram)
+
+    step = 12
     inverse = []
     for k0 in range(0, rank, step):
         height = rank - k0
         heads = [work[j : j + 1, :] for j in range(step)]
         cols = [
-            jnp.broadcast_to(work[:, k0 + j : k0 + j + 1], (height, GRAM_LANES))
-            for j in range(step)
+            jnp.broadcast_to(work[:, k0 + j : k0 + j + 1], (height, LANES)) for j in range(step)
         ]
         scaled = []
         for j in range(step):
@@ -138,22 +133,22 @@
             work = work[step:, :]
             for j in range(step):
                 work = work - cols[j][step:, :] * scaled[j]
-    lower_inverse = jnp.concatenate(inverse, axis=0)
-    lower_inverse = jnp.where(lane >= LOW_LANE, lower_inverse, 0.0)
-
-    wide[...] = jnp.zeros_like(wide)
-    wide[LOW_LANE : LOW_LANE + rank, :] = projected
+    lower_inverse = jnp.where(lane >= HALF, jnp.concatenate(inverse, axis=0), 0.0)
+
+    first = lower_inverse.astype(jnp.bfloat16)
+    second = (lower_inverse - first.astype(jnp.float32)).astype(jnp.bfloat16)
+    above = jnp.zeros((HALF, width), jnp.bfloat16)
+    below = jnp.zeros((LANES - HALF - rank, width), jnp.bfloat16)
     right = jnp.dot(
-        lower_inverse,
-        wide[...],
+        jnp.concatenate([first, second, first], axis=1),
+        jnp.concatenate([above, high, below, above, high, below, above, middle, below], axis=0),
         preferred_element_type=jnp.float32,
-        precision=lax.Precision.HIGHEST,
     )
     right_out[...] = right
     square = right * right
-    folded = square[:, 0:128]
-    for c in range(128, width, 128):
-        folded = folded + square[:, c : c + 128]
+    folded = square[:, 0:LANES]
+    for c in range(LANES, width, LANES):
+        folded = folded + square[:, c : c + LANES]
     folded = jnp.sum(folded, axis=0, keepdims=True)
     norm_out[...] = jnp.broadcast_to(folded, norm_out.shape)
 
@@ -168,7 +163,7 @@
 
 
 def body(theta, gates, edge_weights, sizes, ranks, order, sketch):
-    theta, gates, edge_weights, sketch = theta[0], gates[0], edge_weights[0], sketch[0]
+    theta, edge_weights, sketch = theta[0], edge_weights[0], sketch[0]
     sizes, ranks, order = sizes[0], ranks[0], order[0]
     count, phys, depth, width = theta.shape
     rank = sketch.shape[1]
@@ -186,7 +181,7 @@
             flops=15 * theta.size, bytes_accessed=6 * theta.size, transcendentals=0
         ),
         name="mix",
-    )(jnp.transpose(gates, (1, 2, 0))[:, :, None], theta)
+    )(jnp.transpose(gates, (2, 3, 0, 1)), theta)
     message = pl.pallas_call(
         weigh_kernel,
         out_shape=jax.ShapeDtypeStruct((NEAR, PAIRS, phys, depth, width), theta.dtype),
@@ -198,11 +193,11 @@
     rows_in = lax.all_to_all(
         message, "worker", 0, 0, tiled=True, axis_index_groups=NEAR_GROUPS
     )
-    parts, own = pl.pallas_call(
+    parts, exact = pl.pallas_call(
         contract_kernel,
         out_shape=(
             jax.ShapeDtypeStruct((PAIRS, rank, width), jnp.bfloat16),
-            jax.ShapeDtypeStruct((rank, width), jnp.float32),
+            jax.ShapeDtypeStruct((PAIRS, rank, width), jnp.float32),
         ),
         in_specs=[VMEM, VMEM],
         out_specs=(VMEM, VMEM),
@@ -214,14 +209,13 @@
         solve_kernel,
         out_shape=(
             jax.ShapeDtypeStruct((rank, width), jnp.float32),
-            jax.ShapeDtypeStruct((WORKERS, 128), jnp.float32),
+            jax.ShapeDtypeStruct((WORKERS, LANES), jnp.float32),
         ),
         in_specs=[SMEM, SMEM, SMEM, VMEM, VMEM, VMEM],
         out_specs=(VMEM, VMEM),
-        scratch_shapes=[pltpu.VMEM((GRAM_LANES, width), jnp.float32)],
         compiler_params=pltpu.CompilerParams(vmem_limit_bytes=16 * 2**20),
         name="solve",
-    )(order, sizes, ranks, parts, own, sketch.T)
+    )(order, sizes, ranks, parts, exact, sketch.T)
     norms = lax.all_to_all(norms, "worker", 0, 0, tiled=True)
     factors = pl.pallas_call(
         functools.partial(finish_kernel, float(count)),

time: 82.4 us -> 81.6 us (level)
    unnamed x11 -> x12, local copies, waits for them, and re-layouts: 2.12 us -> 2.11 us
  transfers between devices with their start and end apart: 1 -> 1, of which waited for: 0 -> 0; matrix products, arithmetic and copies ran while one was open for 1% -> 0% of each run, Pallas kernels for 2% -> 2%
where the time goes in v4:
time: 81.6 us; the launch traced here: 81.3 us
  blocking collectives  71.5 us (88%)
  Pallas kernels  5.68 us (7%)
  local copies, waits for them, and re-layouts  2.11 us (3%)
  starting transfers between devices  1.91 us (2%)
    all_to_all x1, blocking collectives, body(): lax.all_to_all(message, 'worker', 0, 0, tiled=True, axis_index_groups=NEA...  28.4 us
    all_to_all x1, blocking collectives, body(): lax.all_to_all(parts, 'worker', 0, 0, tiled=True, axis_index_groups=FAR_G...  25.9 us
    all_to_all x1, blocking collectives, body(): norms = lax.all_to_all(norms, 'worker', 0, 0, tiled=True)  17.2 us
    unnamed x12, local copies, waits for them, and re-layouts  2.11 us
    pallas_call x1, Pallas kernels, body(): pl.pallas_call(solve_kernel, out_shape=(jax.ShapeDtypeStruct((rank, width...  1.93 us
    ppermute x1, starting transfers between devices, body(): lax.ppermute(edge_weights.T, 'stretch', [(i, (i + 1) % stretches) for i i...  1.91 us
  transfers between devices with their start and end apart: 1, of which 0 were waited for; matrix products, arithmetic and copies ran while one was open for 0% of the time, Pallas kernels for 2%

profile of v4, /device:TPU:16, one launch (start us, length us, event | category | flops | bytes accessed | tf_op | source)
XLA Modules:
  0.0 81.3 jit_solution(8475906576338009654)
XLA Ops:
  0.0 1.9 %collective-permute-start = (f32[16,32]{1,0:T(8,128)}, f32[16,32]{1,0:T(8,128)S(1)}, u32[]{:S(2)}, u32[]{:S(2)}) collective-permute-start(f32[16,32]{1,0:T(8,128)} %bitcast.27), channel_id=1, source_target_pairs={{0,32},{32,64},{64,96},{96,128},{128,160},{160,192},{192,224},{224... | collective-permute-start | bytes 6152 | tf_op jit(solution)/shard_map/ppermute | solution.py:171
  1.9 0.0 copy-start
  1.9 1.4 %copy-done = bf16[1,32,3,16,512]{4,3,2,1,0:T(8,128)(2,1)S(1)} copy-done((bf16[1,32,3,16,512]{4,3,2,1,0:T(8,128)(2,1)S(1)}, bf16[1,32,3,16,512]{4,3,2,1,0:T(8,128)(2,1)}, u32[]{:S(2)}) %copy-start) | copy-done | bytes 1572888
  3.3 0.0 copy-start.2
  3.3 0.7 copy-done.2
  4.0 0.0 copy-start.3
  4.0 0.0 copy-start.4
  4.0 1.3 %mix.1.mixed = f32[32,3,16,512]{3,2,1,0:T(8,128)S(1)} custom-call(f32[3,3,1,32]{3,2,1,0:T(1,128)S(1)} %bitcast.21, bf16[32,3,16,512]{3,2,1,0:T(8,128)(2,1)S(1)} %bitcast.16), custom_call_target="tpu_custom_call" | custom-call | flops 11796480 | bytes 4718592 | tf_op jit(solution)/shard_map/mix/pallas_call | solution.py:174
  5.3 0.0 collective-permute-done.left
  5.3 0.0 copy-done.3
  5.3 0.0 copy-done.4
  5.3 0.9 %weigh.1 = bf16[8,4,3,16,512]{4,3,2,1,0:T(8,128)(2,1)S(1)} custom-call(s32[32]{0:T(128)S(1)} %bitcast.22, s32[32]{0:T(128)S(1)} %bitcast.24, f32[32,3,16,512]{3,2,1,0:T(8,128)S(1)} %mix.1.mixed, f32[16,32]{1,0:T(8,128)S(1)} %collective-permute-done.left), custom_call_target="tpu_custom_call" | custom-call | tf_op jit(solution)/shard_map/weigh/pallas_call | solution.py:185
  6.2 0.0 copy-start.1
  6.2 28.4 %all_to_all.21.rows_in = bf16[8,4,3,16,512]{4,3,2,1,0:T(8,128)(2,1)S(1)} all-to-all(bf16[8,4,3,16,512]{4,3,2,1,0:T(8,128)(2,1)S(1)} %weigh.1), channel_id=1, replica_groups={{0,1,8,9,16,17,24,25},{2,3,10,11,18,19,26,27},{4,5,12,13,20,21,28,29},{..., dimensions={0} | all-to-all | bytes 3145728 | tf_op jit(solution)/shard_map/all_to_all | solution.py:193
  34.6 0.0 copy-start.5
  34.6 0.0 copy-done.1
  34.6 0.9 %contract.1 = (bf16[4,48,512]{2,1,0:T(8,128)(2,1)S(1)}, f32[4,48,512]{2,1,0:T(8,128)S(1)}) custom-call(bf16[8,4,3,16,512]{4,3,2,1,0:T(8,128)(2,1)S(1)} %all_to_all.21.rows_in, bf16[48,512]{1,0:T(8,128)(2,1)S(1)} %bitcast.17), custom_call_target="tpu_custom_call" | custom-call | tf_op jit(solution)/shard_map/contract/pallas_call | solution.py:196
  35.5 25.9 %all_to_all.22.parts = bf16[4,48,512]{2,1,0:T(8,128)(2,1)S(1)} all-to-all(bf16[4,48,512]{2,1,0:T(8,128)(2,1)S(1)} %get-tuple-element.9), channel_id=1, replica_groups={{0,2,4,6},{1,3,5,7},{8,10,12,14},{9,11,13,15},{16,18,20,22},{17,19,21,2..., dimensions={0} | all-to-all | bytes 393216 | tf_op jit(solution)/shard_map/all_to_all | solution.py:207
  61.4 0.0 copy-done.5
  61.4 1.9 %solve.1 = (f32[48,512]{1,0:T(8,128)S(1)}, f32[32,128]{1,0:T(8,128)S(1)}) custom-call(s32[32]{0:T(128)S(1)} %bitcast.23, s32[32]{0:T(128)S(1)} %bitcast.25, s32[32]{0:T(128)S(1)} %bitcast.26, bf16[4,48,512]{2,1,0:T(8,128)(2,1)S(1)} %all_to_all.22.parts, f32[4,48,512]{2,1,0:T(8,128)S(1)} %get-tuple-element.10.exact, bf16[48,512]{1,0:T(8,128)(2,1)S(1)} %bitcast.18), custom_call_target="tpu_custom_call" | custom-call | tf_op jit(solution)/shard_map/solve/pallas_call | solution.py:208
  63.4 17.2 %all_to_all.23 = f32[32,1,128]{2,1,0:T(1,128)S(1)} all-to-all(f32[32,1,128]{2,1,0:T(1,128)S(1)} %bitcast.20), channel_id=1, replica_groups=mesh['stretch'=16,'worker'=32] {'worker'}, dimensions={0} | all-to-all | bytes 32768 | tf_op jit(solution)/shard_map/all_to_all | solution.py:219
  80.6 0.7 finish.1
Async XLA Ops:
  0.0 5.3 %collective-permute-start = (f32[16,32]{1,0:T(8,128)}, f32[16,32]{1,0:T(8,128)S(1)}, u32[]{:S(2)}, u32[]{:S(2)}) collective-permute-start(f32[16,32]{1,0:T(8,128)} %bitcast.27), channel_id=1, source_target_pairs={{0,32},{32,64},{64,96},{96,128},{128,160},{160,192},{192,224},{224... | collective-permute-start | bytes 6152 | tf_op jit(solution)/shard_map/ppermute | solution.py:171
  1.9 1.4 %copy-start = (bf16[1,32,3,16,512]{4,3,2,1,0:T(8,128)(2,1)S(1)}, bf16[1,32,3,16,512]{4,3,2,1,0:T(8,128)(2,1)}, u32[]{:S(2)}) copy-start(bf16[1,32,3,16,512]{4,3,2,1,0:T(8,128)(2,1)} %param.7) | copy-start | bytes 4718596
  3.3 0.7 copy-start.2
  4.0 1.3 %copy-start.3 = (s32[1,32]{1,0:T(1,128)S(1)}, s32[1,32]{1,0:T(1,128)}, u32[]{:S(2)}) copy-start(s32[1,32]{1,0:T(1,128)} %param.12) | copy-start | bytes 388
  4.0 1.3 %copy-start.4 = (s32[1,32]{1,0:T(1,128)S(1)}, s32[1,32]{1,0:T(1,128)}, u32[]{:S(2)}) copy-start(s32[1,32]{1,0:T(1,128)} %param.10) | copy-start | bytes 388
  6.2 28.4 %copy-start.1 = (bf16[1,512,48]{1,2,0:T(8,128)(2,1)S(1)}, bf16[1,512,48]{1,2,0:T(8,128)(2,1)}, u32[]{:S(2)}) copy-start(bf16[1,512,48]{1,2,0:T(8,128)(2,1)} %param.13) | copy-start | bytes 147460
  34.6 26.8 %copy-start.5 = (s32[1,32]{1,0:T(1,128)S(1)}, s32[1,32]{1,0:T(1,128)}, u32[]{:S(2)}) copy-start(s32[1,32]{1,0:T(1,128)} %param.11) | copy-start | bytes 388

commit v5 on v4

--- a/solution.py
+++ b/solution.py
@@ -16,6 +16,7 @@
 FAR_GROUPS = [[x * NZ + 2 * p + q for p in range(PAIRS)] for x in range(NX) for q in range(2)]
 LANES = 128
 HALF = 64
+COST = 100
 OVER_LANES = (((1,), (1,)), ((), ()))
 
 
@@ -54,34 +55,26 @@
                 message[d, j, g] = rows.astype(jnp.bfloat16)
 
 
-def contract_kernel(rows_in, sketch, out, exact):
-    near, pairs, phys, depth, width = rows_in.shape
-    basis = sketch[...]
-
-    def rows_of(j):
-        return rows_in[:, j].reshape(near * phys * depth, width)
-
-    samples = [
-        lax.dot_general(basis, rows_of(j), OVER_LANES, preferred_element_type=jnp.float32)
-        for j in range(pairs)
-    ]
-    for j in range(pairs):
-        projected = jnp.dot(
-            samples[j].astype(jnp.bfloat16), rows_of(j), preferred_element_type=jnp.float32
-        )
-        out[j] = projected.astype(jnp.bfloat16)
-        exact[j] = projected
-
-
-def solve_kernel(order, sizes, ranks, parts, exact, sketch, right_out, norm_out):
-    me, _, pair, _ = place()
-    pairs, rank, width = parts.shape
+def contract_kernel(flip, rows_in, sketch, *refs):
+    near, _, phys, depth, width = rows_in.shape
+    out = refs[-1]
+    rows = rows_in[:, place()[2] ^ flip].reshape(near * phys * depth, width)
+    sample = lax.dot_general(
+        sketch[...], rows, OVER_LANES, preferred_element_type=jnp.float32
+    )
+    projected = jnp.dot(sample.astype(jnp.bfloat16), rows, preferred_element_type=jnp.float32)
+    out[...] = projected.astype(out.dtype)
+
+
+def solve_kernel(order, sizes, ranks, exact, part1, part2, part3, sketch, right_out, norm_out):
+    me = place()[0]
+    rank, width = exact.shape
     blk = order[me]
     kept = jnp.minimum(ranks[blk], sizes[blk] // 2)
 
-    projected = exact[pair]
-    for p in range(pairs):
-        projected = projected + jnp.where(pair == p, 0.0, parts[p].astype(jnp.float32))
+    projected = exact[...]
+    for part in (part1, part2, part3):
+        projected = projected + part[...].astype(jnp.float32)
     prow = lax.broadcasted_iota(jnp.int32, (rank, width), 0)
     projected = jnp.where(prow < kept, projected, 0.0)
     high = projected.astype(jnp.bfloat16)
@@ -193,29 +186,36 @@
     rows_in = lax.all_to_all(
         message, "worker", 0, 0, tiled=True, axis_index_groups=NEAR_GROUPS
     )
-    parts, exact = pl.pallas_call(
-        contract_kernel,
-        out_shape=(
-            jax.ShapeDtypeStruct((PAIRS, rank, width), jnp.bfloat16),
-            jax.ShapeDtypeStruct((PAIRS, rank, width), jnp.float32),
-        ),
-        in_specs=[VMEM, VMEM],
-        out_specs=(VMEM, VMEM),
-        compiler_params=pltpu.CompilerParams(vmem_limit_bytes=16 * 2**20),
-        name="contract",
-    )(rows_in, sketch.T)
-    parts = lax.all_to_all(parts, "worker", 0, 0, tiled=True, axis_index_groups=FAR_GROUPS)
+    parts = {}
+    made = ()
+    for flip in (2, 3, 1, 0):
+        part = pl.pallas_call(
+            functools.partial(contract_kernel, flip),
+            out_shape=jax.ShapeDtypeStruct((rank, width), jnp.bfloat16 if flip else jnp.float32),
+            in_specs=[VMEM, VMEM] + [VMEM] * len(made),
+            out_specs=VMEM,
+            compiler_params=pltpu.CompilerParams(vmem_limit_bytes=16 * 2**20),
+            cost_estimate=pl.CostEstimate(
+                flops=COST * rows_in.size, bytes_accessed=COST * rows_in.size, transcendentals=0
+            ),
+            name=f"contract{flip}",
+        )(rows_in, sketch.T, *made)
+        made = (part,)
+        if flip:
+            part = lax.ppermute(part, "worker", [(w, w ^ (2 * flip)) for w in range(WORKERS)])
+        parts[flip] = part
+    exact = parts[0]
     right, norms = pl.pallas_call(
         solve_kernel,
         out_shape=(
             jax.ShapeDtypeStruct((rank, width), jnp.float32),
             jax.ShapeDtypeStruct((WORKERS, LANES), jnp.float32),
         ),
-        in_specs=[SMEM, SMEM, SMEM, VMEM, VMEM, VMEM],
+        in_specs=[SMEM, SMEM, SMEM] + [VMEM] * 5,
         out_specs=(VMEM, VMEM),
         compiler_params=pltpu.CompilerParams(vmem_limit_bytes=16 * 2**20),
         name="solve",
-    )(order, sizes, ranks, parts, exact, sketch.T)
+    )(order, sizes, ranks, exact, parts[1], parts[2], parts[3], sketch.T)
     norms = lax.all_to_all(norms, "worker", 0, 0, tiled=True)
     factors = pl.pallas_call(
         functools.partial(finish_kernel, float(count)),

time: 81.6 us -> 83 us (1.017)
  blocking collectives: 71.5 us -> 46.2 us
  starting transfers between devices: 1.91 us -> 18.1 us
  waiting for transfers between devices: 0.01 us -> 9.51 us
  Pallas kernels: 5.68 us -> 6.59 us
    all_to_all x1 -> x0, blocking collectives: 25.9 us -> none  [body(): lax.all_to_all(parts, 'worker', 0, 0, tiled=True, axis_index_groups=FAR_G...]
    ppermute x0 -> x3, starting transfers between devices: none -> 16.2 us  [body(): lax.ppermute(part, 'worker', [(w, w ^ 2 * flip) for w in range(WORKERS)])]
    ppermute x0 -> x3, waiting for transfers between devices: none -> 9.51 us  [body(): lax.ppermute(part, 'worker', [(w, w ^ 2 * flip) for w in range(WORKERS)])]
    pallas_call x1 -> x4, Pallas kernels: 0.85 us -> 1.78 us  [body(): pl.pallas_call(functools.partial(contract_kernel, flip), out_shape=jax.Sh...]
  transfers between devices with their start and end apart: 1 -> 4, of which waited for: 0 -> 2; matrix products, arithmetic and copies ran while one was open for 0% -> 0% of each run, Pallas kernels for 2% -> 2%
where the time goes in v5:
time: 83 us; the launch traced here: 82.6 us
  blocking collectives  46.2 us (56%)
  starting transfers between devices  18.1 us (22%)
  waiting for transfers between devices  9.51 us (11%)
  Pallas kernels  6.59 us (8%)
  local copies, waits for them, and re-layouts  2.11 us (3%)
    all_to_all x1, blocking collectives, body(): lax.all_to_all(message, 'worker', 0, 0, tiled=True, axis_index_groups=NEA...  28.4 us
    all_to_all x1, blocking collectives, body(): norms = lax.all_to_all(norms, 'worker', 0, 0, tiled=True)  17.8 us
    ppermute x3, starting transfers between devices, body(): lax.ppermute(part, 'worker', [(w, w ^ 2 * flip) for w in range(WORKERS)])  16.2 us
    ppermute x3, waiting for transfers between devices, body(): lax.ppermute(part, 'worker', [(w, w ^ 2 * flip) for w in range(WORKERS)])  9.51 us
    unnamed x12, local copies, waits for them, and re-layouts  2.11 us
    pallas_call x1, Pallas kernels, body(): pl.pallas_call(solve_kernel, out_shape=(jax.ShapeDtypeStruct((rank, width...  1.91 us
    ppermute x1, starting transfers between devices, body(): lax.ppermute(edge_weights.T, 'stretch', [(i, (i + 1) % stretches) for i i...  1.91 us
    pallas_call x4, Pallas kernels, body(): pl.pallas_call(functools.partial(contract_kernel, flip), out_shape=jax.Sh...  1.78 us
  transfers between devices with their start and end apart: 4, of which 2 were waited for; matrix products, arithmetic and copies ran while one was open for 0% of the time, Pallas kernels for 2%

profile of v5, /device:TPU:16, one launch (start us, length us, event | category | flops | bytes accessed | tf_op | source)
XLA Modules:
  0.0 82.6 jit_solution(7528113664178817802)
XLA Ops:
  0.0 1.9 %collective-permute-start = (f32[16,32]{1,0:T(8,128)}, f32[16,32]{1,0:T(8,128)S(1)}, u32[]{:S(2)}, u32[]{:S(2)}) collective-permute-start(f32[16,32]{1,0:T(8,128)} %bitcast.30), channel_id=1, source_target_pairs={{0,32},{32,64},{64,96},{96,128},{128,160},{160,192},{192,224},{224... | collective-permute-start | bytes 6152 | tf_op jit(solution)/shard_map/ppermute | solution.py:164
  1.9 0.0 copy-start
  1.9 1.4 %copy-done = bf16[1,32,3,16,512]{4,3,2,1,0:T(8,128)(2,1)S(1)} copy-done((bf16[1,32,3,16,512]{4,3,2,1,0:T(8,128)(2,1)S(1)}, bf16[1,32,3,16,512]{4,3,2,1,0:T(8,128)(2,1)}, u32[]{:S(2)}) %copy-start) | copy-done | bytes 1572888
  3.3 0.0 copy-start.2
  3.3 0.7 copy-done.2
  4.0 0.0 copy-start.3
  4.0 0.0 copy-start.4
  4.0 1.3 %mix.1.mixed = f32[32,3,16,512]{3,2,1,0:T(8,128)S(1)} custom-call(f32[3,3,1,32]{3,2,1,0:T(1,128)S(1)} %bitcast.24, bf16[32,3,16,512]{3,2,1,0:T(8,128)(2,1)S(1)} %bitcast.16), custom_call_target="tpu_custom_call" | custom-call | flops 11796480 | bytes 4718592 | tf_op jit(solution)/shard_map/mix/pallas_call | solution.py:167
  5.3 0.0 collective-permute-done.left
  5.3 0.0 copy-done.3
  5.3 0.0 copy-done.4
  5.3 0.9 %weigh.1 = bf16[8,4,3,16,512]{4,3,2,1,0:T(8,128)(2,1)S(1)} custom-call(s32[32]{0:T(128)S(1)} %bitcast.25, s32[32]{0:T(128)S(1)} %bitcast.27, f32[32,3,16,512]{3,2,1,0:T(8,128)S(1)} %mix.1.mixed, f32[16,32]{1,0:T(8,128)S(1)} %collective-permute-done.left), custom_call_target="tpu_custom_call" | custom-call | tf_op jit(solution)/shard_map/weigh/pallas_call | solution.py:178
  6.2 0.0 copy-start.1
  6.2 28.4 %all_to_all.16.rows_in = bf16[8,4,3,16,512]{4,3,2,1,0:T(8,128)(2,1)S(1)} all-to-all(bf16[8,4,3,16,512]{4,3,2,1,0:T(8,128)(2,1)S(1)} %weigh.1), channel_id=1, replica_groups={{0,1,8,9,16,17,24,25},{2,3,10,11,18,19,26,27},{4,5,12,13,20,21,28,29},{..., dimensions={0} | all-to-all | bytes 3145728 | tf_op jit(solution)/shard_map/all_to_all | solution.py:186
  34.6 0.0 copy-done.1
  34.6 0.4 contract2.1.refs_0_
  35.1 0.5 contract3.1.refs_0_
  35.5 0.0 copy-start.5
  35.5 0.4 contract1.1.refs_0_
  36.0 5.2 %collective-permute-start.1 = (bf16[48,512]{1,0:T(8,128)(2,1)S(1)}, bf16[48,512]{1,0:T(8,128)(2,1)S(1)}, u32[]{:S(2)}, u32[]{:S(2)}) collective-permute-start(bf16[48,512]{1,0:T(8,128)(2,1)S(1)} %contract1.1.refs_0_), channel_id=1, source_target_pairs={{0,2},{1,3},{2,0},{3,1},{4,6},{5,7},{6,4},{7,5},{8,10},{9,11},{10,... | collective-permute-start | bytes 147464 | tf_op jit(solution)/shard_map/ppermute | solution.py:205
  41.2 8.5 %collective-permute-start.3 = (bf16[48,512]{1,0:T(8,128)(2,1)S(1)}, bf16[48,512]{1,0:T(8,128)(2,1)S(1)}, u32[]{:S(2)}, u32[]{:S(2)}) collective-permute-start(bf16[48,512]{1,0:T(8,128)(2,1)S(1)} %contract3.1.refs_0_), channel_id=1, source_target_pairs={{0,6},{1,7},{2,4},{3,5},{4,2},{5,3},{6,0},{7,1},{8,14},{9,15},{10,... | collective-permute-start | bytes 147464 | tf_op jit(solution)/shard_map/ppermute | solution.py:205
  49.7 2.5 %collective-permute-start.2 = (bf16[48,512]{1,0:T(8,128)(2,1)S(1)}, bf16[48,512]{1,0:T(8,128)(2,1)S(1)}, u32[]{:S(2)}, u32[]{:S(2)}) collective-permute-start(bf16[48,512]{1,0:T(8,128)(2,1)S(1)} %contract2.1.refs_0_), channel_id=1, source_target_pairs={{0,4},{1,5},{2,6},{3,7},{4,0},{5,1},{6,2},{7,3},{8,12},{9,13},{10,... | collective-permute-start | bytes 147464 | tf_op jit(solution)/shard_map/ppermute | solution.py:205
  52.2 0.5 contract0.1.exact
  52.7 0.0 collective-permute-done.1.part1
  52.7 0.8 %collective-permute-done.3.part3 = bf16[48,512]{1,0:T(8,128)(2,1)S(1)} collective-permute-done((bf16[48,512]{1,0:T(8,128)(2,1)S(1)}, bf16[48,512]{1,0:T(8,128)(2,1)S(1)}, u32[]{:S(2)}, u32[]{:S(2)}) %collective-permute-start.3) | collective-permute-done | bytes 49184 | tf_op jit(solution)/shard_map/ppermute | solution.py:205
  53.5 8.7 %collective-permute-done.2.part2 = bf16[48,512]{1,0:T(8,128)(2,1)S(1)} collective-permute-done((bf16[48,512]{1,0:T(8,128)(2,1)S(1)}, bf16[48,512]{1,0:T(8,128)(2,1)S(1)}, u32[]{:S(2)}, u32[]{:S(2)}) %collective-permute-start.2) | collective-permute-done | bytes 49184 | tf_op jit(solution)/shard_map/ppermute | solution.py:205
  62.2 0.0 copy-done.5
  62.2 1.9 %solve.1 = (f32[48,512]{1,0:T(8,128)S(1)}, f32[32,128]{1,0:T(8,128)S(1)}) custom-call(s32[32]{0:T(128)S(1)} %bitcast.26, s32[32]{0:T(128)S(1)} %bitcast.28, s32[32]{0:T(128)S(1)} %bitcast.29, f32[48,512]{1,0:T(8,128)S(1)} %contract0.1.exact, bf16[48,512]{1,0:T(8,128)(2,1)S(1)} %collective-permute-done.1.part1, ...), custom_call_target="tpu_custom_call" | custom-call | tf_op jit(solution)/shard_map/solve/pallas_call | solution.py:208
  64.1 17.8 %all_to_all.17 = f32[32,1,128]{2,1,0:T(1,128)S(1)} all-to-all(f32[32,1,128]{2,1,0:T(1,128)S(1)} %bitcast.23), channel_id=1, replica_groups=mesh['stretch'=16,'worker'=32] {'worker'}, dimensions={0} | all-to-all | bytes 32768 | tf_op jit(solution)/shard_map/all_to_all | solution.py:219
  81.9 0.7 finish.1
Async XLA Ops:
  0.0 5.3 %collective-permute-start = (f32[16,32]{1,0:T(8,128)}, f32[16,32]{1,0:T(8,128)S(1)}, u32[]{:S(2)}, u32[]{:S(2)}) collective-permute-start(f32[16,32]{1,0:T(8,128)} %bitcast.30), channel_id=1, source_target_pairs={{0,32},{32,64},{64,96},{96,128},{128,160},{160,192},{192,224},{224... | collective-permute-start | bytes 6152 | tf_op jit(solution)/shard_map/ppermute | solution.py:164
  1.9 1.4 %copy-start = (bf16[1,32,3,16,512]{4,3,2,1,0:T(8,128)(2,1)S(1)}, bf16[1,32,3,16,512]{4,3,2,1,0:T(8,128)(2,1)}, u32[]{:S(2)}) copy-start(bf16[1,32,3,16,512]{4,3,2,1,0:T(8,128)(2,1)} %param.7) | copy-start | bytes 4718596
  3.3 0.7 copy-start.2
  4.0 1.3 %copy-start.3 = (s32[1,32]{1,0:T(1,128)S(1)}, s32[1,32]{1,0:T(1,128)}, u32[]{:S(2)}) copy-start(s32[1,32]{1,0:T(1,128)} %param.12) | copy-start | bytes 388
  4.0 1.3 %copy-start.4 = (s32[1,32]{1,0:T(1,128)S(1)}, s32[1,32]{1,0:T(1,128)}, u32[]{:S(2)}) copy-start(s32[1,32]{1,0:T(1,128)} %param.10) | copy-start | bytes 388
  6.2 28.4 %copy-start.1 = (bf16[1,512,48]{1,2,0:T(8,128)(2,1)S(1)}, bf16[1,512,48]{1,2,0:T(8,128)(2,1)}, u32[]{:S(2)}) copy-start(bf16[1,512,48]{1,2,0:T(8,128)(2,1)} %param.13) | copy-start | bytes 147460
  35.5 26.6 %copy-start.5 = (s32[1,32]{1,0:T(1,128)S(1)}, s32[1,32]{1,0:T(1,128)}, u32[]{:S(2)}) copy-start(s32[1,32]{1,0:T(1,128)} %param.11) | copy-start | bytes 388
  36.0 16.7 %collective-permute-start.1 = (bf16[48,512]{1,0:T(8,128)(2,1)S(1)}, bf16[48,512]{1,0:T(8,128)(2,1)S(1)}, u32[]{:S(2)}, u32[]{:S(2)}) collective-permute-start(bf16[48,512]{1,0:T(8,128)(2,1)S(1)} %contract1.1.refs_0_), channel_id=1, source_target_pairs={{0,2},{1,3},{2,0},{3,1},{4,6},{5,7},{6,4},{7,5},{8,10},{9,11},{10,... | collective-permute-start | bytes 147464 | tf_op jit(solution)/shard_map/ppermute | solution.py:205
  41.2 12.3 %collective-permute-start.3 = (bf16[48,512]{1,0:T(8,128)(2,1)S(1)}, bf16[48,512]{1,0:T(8,128)(2,1)S(1)}, u32[]{:S(2)}, u32[]{:S(2)}) collective-permute-start(bf16[48,512]{1,0:T(8,128)(2,1)S(1)} %contract3.1.refs_0_), channel_id=1, source_target_pairs={{0,6},{1,7},{2,4},{3,5},{4,2},{5,3},{6,0},{7,1},{8,14},{9,15},{10,... | collective-permute-start | bytes 147464 | tf_op jit(solution)/shard_map/ppermute | solution.py:205
  49.7 12.4 %collective-permute-start.2 = (bf16[48,512]{1,0:T(8,128)(2,1)S(1)}, bf16[48,512]{1,0:T(8,128)(2,1)S(1)}, u32[]{:S(2)}, u32[]{:S(2)}) collective-permute-start(bf16[48,512]{1,0:T(8,128)(2,1)S(1)} %contract2.1.refs_0_), channel_id=1, source_target_pairs={{0,4},{1,5},{2,6},{3,7},{4,0},{5,1},{6,2},{7,3},{8,12},{9,13},{10,... | collective-permute-start | bytes 147464 | tf_op jit(solution)/shard_map/ppermute | solution.py:205

commit v6 on v4

--- a/solution.py
+++ b/solution.py
@@ -12,7 +12,8 @@
 PAIRS = NZ // 2
 NEAR = NX * 2
 WORKERS = NX * NZ
-NEAR_GROUPS = [[x * NZ + 2 * p + q for x in range(NX) for q in range(2)] for p in range(PAIRS)]
+NEAR_ORDER = [(0, 0), (0, 1), (1, 1), (1, 0), (2, 0), (2, 1), (3, 1), (3, 0)]
+NEAR_GROUPS = [[x * NZ + 2 * p + q for x, q in NEAR_ORDER] for p in range(PAIRS)]
 FAR_GROUPS = [[x * NZ + 2 * p + q for p in range(PAIRS)] for x in range(NX) for q in range(2)]
 LANES = 128
 HALF = 64
@@ -45,7 +46,7 @@
     bond = lax.broadcasted_iota(jnp.int32, (1, width), 1)
     for d in range(NEAR):
         for j in range(PAIRS):
-            blk = order[(d // 2) * NZ + 2 * j + d % 2]
+            blk = order[NEAR_ORDER[d][0] * NZ + 2 * j + NEAR_ORDER[d][1]]
             size = sizes[blk]
             scale = jnp.sum(jnp.where(lane == blk, columns, 0.0), axis=1, keepdims=True)
             scale = jnp.where(row < size, scale, 0.0)

time: 81.6 us -> 81.4 us (level)
    all_to_all x1, blocking collectives: 17.2 us -> 18.6 us  [body(): norms = lax.all_to_all(norms, 'worker', 0, 0, tiled=True)]
    all_to_all x1, blocking collectives: 28.4 us -> 27.6 us  [body(): lax.all_to_all(message, 'worker', 0, 0, tiled=True, axis_index_groups=NEA...]
where the time goes in v6:
time: 81.4 us; the launch traced here: 81.1 us
  blocking collectives  71.3 us (88%)
  Pallas kernels  5.67 us (7%)
  local copies, waits for them, and re-layouts  2.11 us (3%)
  starting transfers between devices  1.91 us (2%)
    all_to_all x1, blocking collectives, body(): lax.all_to_all(message, 'worker', 0, 0, tiled=True, axis_index_groups=NEA...  27.6 us
    all_to_all x1, blocking collectives, body(): lax.all_to_all(parts, 'worker', 0, 0, tiled=True, axis_index_groups=FAR_G...  25.2 us
    all_to_all x1, blocking collectives, body(): norms = lax.all_to_all(norms, 'worker', 0, 0, tiled=True)  18.6 us
    unnamed x12, local copies, waits for them, and re-layouts  2.11 us
    pallas_call x1, Pallas kernels, body(): pl.pallas_call(solve_kernel, out_shape=(jax.ShapeDtypeStruct((rank, width...  1.93 us
    ppermute x1, starting transfers between devices, body(): lax.ppermute(edge_weights.T, 'stretch', [(i, (i + 1) % stretches) for i i...  1.91 us
  transfers between devices with their start and end apart: 1, of which 0 were waited for; matrix products, arithmetic and copies ran while one was open for 0% of the time, Pallas kernels for 2%

profile of v6, /device:TPU:16, one launch (start us, length us, event | category | flops | bytes accessed | tf_op | source)
XLA Modules:
  0.0 81.1 jit_solution(10095458256500370081)
XLA Ops:
  0.0 1.9 %collective-permute-start = (f32[16,32]{1,0:T(8,128)}, f32[16,32]{1,0:T(8,128)S(1)}, u32[]{:S(2)}, u32[]{:S(2)}) collective-permute-start(f32[16,32]{1,0:T(8,128)} %bitcast.27), channel_id=1, source_target_pairs={{0,32},{32,64},{64,96},{96,128},{128,160},{160,192},{192,224},{224... | collective-permute-start | bytes 6152 | tf_op jit(solution)/shard_map/ppermute | solution.py:172
  1.9 0.0 copy-start
  1.9 1.4 %copy-done = bf16[1,32,3,16,512]{4,3,2,1,0:T(8,128)(2,1)S(1)} copy-done((bf16[1,32,3,16,512]{4,3,2,1,0:T(8,128)(2,1)S(1)}, bf16[1,32,3,16,512]{4,3,2,1,0:T(8,128)(2,1)}, u32[]{:S(2)}) %copy-start) | copy-done | bytes 1572888
  3.3 0.0 copy-start.2
  3.3 0.7 copy-done.2
  4.0 0.0 copy-start.3
  4.0 0.0 copy-start.4
  4.0 1.3 %mix.1.mixed = f32[32,3,16,512]{3,2,1,0:T(8,128)S(1)} custom-call(f32[3,3,1,32]{3,2,1,0:T(1,128)S(1)} %bitcast.21, bf16[32,3,16,512]{3,2,1,0:T(8,128)(2,1)S(1)} %bitcast.16), custom_call_target="tpu_custom_call" | custom-call | flops 11796480 | bytes 4718592 | tf_op jit(solution)/shard_map/mix/pallas_call | solution.py:175
  5.3 0.0 collective-permute-done.left
  5.3 0.0 copy-done.3
  5.3 0.0 copy-done.4
  5.3 0.9 %weigh.1 = bf16[8,4,3,16,512]{4,3,2,1,0:T(8,128)(2,1)S(1)} custom-call(s32[32]{0:T(128)S(1)} %bitcast.22, s32[32]{0:T(128)S(1)} %bitcast.24, f32[32,3,16,512]{3,2,1,0:T(8,128)S(1)} %mix.1.mixed, f32[16,32]{1,0:T(8,128)S(1)} %collective-permute-done.left), custom_call_target="tpu_custom_call" | custom-call | tf_op jit(solution)/shard_map/weigh/pallas_call | solution.py:186
  6.2 0.0 copy-start.1
  6.2 27.6 %all_to_all.21.rows_in = bf16[8,4,3,16,512]{4,3,2,1,0:T(8,128)(2,1)S(1)} all-to-all(bf16[8,4,3,16,512]{4,3,2,1,0:T(8,128)(2,1)S(1)} %weigh.1), channel_id=1, replica_groups={{0,1,9,8,16,17,25,24},{2,3,11,10,18,19,27,26},{4,5,13,12,20,21,29,28},{..., dimensions={0} | all-to-all | bytes 3145728 | tf_op jit(solution)/shard_map/all_to_all | solution.py:194
  33.8 0.0 copy-start.5
  33.8 0.0 copy-done.1
  33.8 0.8 %contract.1 = (bf16[4,48,512]{2,1,0:T(8,128)(2,1)S(1)}, f32[4,48,512]{2,1,0:T(8,128)S(1)}) custom-call(bf16[8,4,3,16,512]{4,3,2,1,0:T(8,128)(2,1)S(1)} %all_to_all.21.rows_in, bf16[48,512]{1,0:T(8,128)(2,1)S(1)} %bitcast.17), custom_call_target="tpu_custom_call" | custom-call | tf_op jit(solution)/shard_map/contract/pallas_call | solution.py:197
  34.7 25.2 %all_to_all.22.parts = bf16[4,48,512]{2,1,0:T(8,128)(2,1)S(1)} all-to-all(bf16[4,48,512]{2,1,0:T(8,128)(2,1)S(1)} %get-tuple-element.9), channel_id=1, replica_groups={{0,2,4,6},{1,3,5,7},{8,10,12,14},{9,11,13,15},{16,18,20,22},{17,19,21,2..., dimensions={0} | all-to-all | bytes 393216 | tf_op jit(solution)/shard_map/all_to_all | solution.py:208
  59.8 0.0 copy-done.5
  59.8 1.9 %solve.1 = (f32[48,512]{1,0:T(8,128)S(1)}, f32[32,128]{1,0:T(8,128)S(1)}) custom-call(s32[32]{0:T(128)S(1)} %bitcast.23, s32[32]{0:T(128)S(1)} %bitcast.25, s32[32]{0:T(128)S(1)} %bitcast.26, bf16[4,48,512]{2,1,0:T(8,128)(2,1)S(1)} %all_to_all.22.parts, f32[4,48,512]{2,1,0:T(8,128)S(1)} %get-tuple-element.10.exact, bf16[48,512]{1,0:T(8,128)(2,1)S(1)} %bitcast.18), custom_call_target="tpu_custom_call" | custom-call | tf_op jit(solution)/shard_map/solve/pallas_call | solution.py:209
  61.8 18.6 %all_to_all.23 = f32[32,1,128]{2,1,0:T(1,128)S(1)} all-to-all(f32[32,1,128]{2,1,0:T(1,128)S(1)} %bitcast.20), channel_id=1, replica_groups=mesh['stretch'=16,'worker'=32] {'worker'}, dimensions={0} | all-to-all | bytes 32768 | tf_op jit(solution)/shard_map/all_to_all | solution.py:220
  80.4 0.7 finish.1
Async XLA Ops:
  0.0 5.3 %collective-permute-start = (f32[16,32]{1,0:T(8,128)}, f32[16,32]{1,0:T(8,128)S(1)}, u32[]{:S(2)}, u32[]{:S(2)}) collective-permute-start(f32[16,32]{1,0:T(8,128)} %bitcast.27), channel_id=1, source_target_pairs={{0,32},{32,64},{64,96},{96,128},{128,160},{160,192},{192,224},{224... | collective-permute-start | bytes 6152 | tf_op jit(solution)/shard_map/ppermute | solution.py:172
  1.9 1.4 %copy-start = (bf16[1,32,3,16,512]{4,3,2,1,0:T(8,128)(2,1)S(1)}, bf16[1,32,3,16,512]{4,3,2,1,0:T(8,128)(2,1)}, u32[]{:S(2)}) copy-start(bf16[1,32,3,16,512]{4,3,2,1,0:T(8,128)(2,1)} %param.7) | copy-start | bytes 4718596
  3.3 0.7 copy-start.2
  4.0 1.3 %copy-start.3 = (s32[1,32]{1,0:T(1,128)S(1)}, s32[1,32]{1,0:T(1,128)}, u32[]{:S(2)}) copy-start(s32[1,32]{1,0:T(1,128)} %param.12) | copy-start | bytes 388
  4.0 1.3 %copy-start.4 = (s32[1,32]{1,0:T(1,128)S(1)}, s32[1,32]{1,0:T(1,128)}, u32[]{:S(2)}) copy-start(s32[1,32]{1,0:T(1,128)} %param.10) | copy-start | bytes 388
  6.2 27.6 %copy-start.1 = (bf16[1,512,48]{1,2,0:T(8,128)(2,1)S(1)}, bf16[1,512,48]{1,2,0:T(8,128)(2,1)}, u32[]{:S(2)}) copy-start(bf16[1,512,48]{1,2,0:T(8,128)(2,1)} %param.13) | copy-start | bytes 147460
  33.8 26.0 %copy-start.5 = (s32[1,32]{1,0:T(1,128)S(1)}, s32[1,32]{1,0:T(1,128)}, u32[]{:S(2)}) copy-start(s32[1,32]{1,0:T(1,128)} %param.11) | copy-start | bytes 388

commit v7 on v6

--- a/solution.py
+++ b/solution.py
@@ -81,8 +81,8 @@
     kept = jnp.minimum(ranks[blk], sizes[blk] // 2)
 
     projected = exact[pair]
-    for p in range(pairs):
-        projected = projected + jnp.where(pair == p, 0.0, parts[p].astype(jnp.float32))
+    for flip in range(1, pairs):
+        projected = projected + parts[pair ^ flip].astype(jnp.float32)
     prow = lax.broadcasted_iota(jnp.int32, (rank, width), 0)
     projected = jnp.where(prow < kept, projected, 0.0)
     high = projected.astype(jnp.bfloat16)

time: 81.4 us -> 81.4 us (level)
  no operation moved by 1% of the time
where the time goes in v7:
time: 81.4 us; the launch traced here: 81.1 us
  blocking collectives  71.3 us (88%)
  Pallas kernels  5.67 us (7%)
  local copies, waits for them, and re-layouts  2.11 us (3%)
  starting transfers between devices  1.91 us (2%)
    all_to_all x1, blocking collectives, body(): lax.all_to_all(message, 'worker', 0, 0, tiled=True, axis_index_groups=NEA...  27.6 us
    all_to_all x1, blocking collectives, body(): lax.all_to_all(parts, 'worker', 0, 0, tiled=True, axis_index_groups=FAR_G...  25.2 us
    all_to_all x1, blocking collectives, body(): norms = lax.all_to_all(norms, 'worker', 0, 0, tiled=True)  18.6 us
    unnamed x12, local copies, waits for them, and re-layouts  2.11 us
    pallas_call x1, Pallas kernels, body(): pl.pallas_call(solve_kernel, out_shape=(jax.ShapeDtypeStruct((rank, width...  1.93 us
    ppermute x1, starting transfers between devices, body(): lax.ppermute(edge_weights.T, 'stretch', [(i, (i + 1) % stretches) for i i...  1.91 us
  transfers between devices with their start and end apart: 1, of which 0 were waited for; matrix products, arithmetic and copies ran while one was open for 0% of the time, Pallas kernels for 2%

profile of v7, /device:TPU:16, one launch (start us, length us, event | category | flops | bytes accessed | tf_op | source)
XLA Modules:
  0.0 81.1 jit_solution(9707649198026060998)
XLA Ops:
  0.0 1.9 %collective-permute-start = (f32[16,32]{1,0:T(8,128)}, f32[16,32]{1,0:T(8,128)S(1)}, u32[]{:S(2)}, u32[]{:S(2)}) collective-permute-start(f32[16,32]{1,0:T(8,128)} %bitcast.27), channel_id=1, source_target_pairs={{0,32},{32,64},{64,96},{96,128},{128,160},{160,192},{192,224},{224... | collective-permute-start | bytes 6152 | tf_op jit(solution)/shard_map/ppermute | solution.py:172
  1.9 0.0 copy-start
  1.9 1.4 %copy-done = bf16[1,32,3,16,512]{4,3,2,1,0:T(8,128)(2,1)S(1)} copy-done((bf16[1,32,3,16,512]{4,3,2,1,0:T(8,128)(2,1)S(1)}, bf16[1,32,3,16,512]{4,3,2,1,0:T(8,128)(2,1)}, u32[]{:S(2)}) %copy-start) | copy-done | bytes 1572888
  3.3 0.0 copy-start.2
  3.3 0.7 copy-done.2
  4.0 0.0 copy-start.3
  4.0 0.0 copy-start.4
  4.0 1.3 %mix.1.mixed = f32[32,3,16,512]{3,2,1,0:T(8,128)S(1)} custom-call(f32[3,3,1,32]{3,2,1,0:T(1,128)S(1)} %bitcast.21, bf16[32,3,16,512]{3,2,1,0:T(8,128)(2,1)S(1)} %bitcast.16), custom_call_target="tpu_custom_call" | custom-call | flops 11796480 | bytes 4718592 | tf_op jit(solution)/shard_map/mix/pallas_call | solution.py:175
  5.3 0.0 collective-permute-done.left
  5.3 0.0 copy-done.3
  5.3 0.0 copy-done.4
  5.3 0.9 %weigh.1 = bf16[8,4,3,16,512]{4,3,2,1,0:T(8,128)(2,1)S(1)} custom-call(s32[32]{0:T(128)S(1)} %bitcast.22, s32[32]{0:T(128)S(1)} %bitcast.24, f32[32,3,16,512]{3,2,1,0:T(8,128)S(1)} %mix.1.mixed, f32[16,32]{1,0:T(8,128)S(1)} %collective-permute-done.left), custom_call_target="tpu_custom_call" | custom-call | tf_op jit(solution)/shard_map/weigh/pallas_call | solution.py:186
  6.2 0.0 copy-start.1
  6.2 27.6 %all_to_all.21.rows_in = bf16[8,4,3,16,512]{4,3,2,1,0:T(8,128)(2,1)S(1)} all-to-all(bf16[8,4,3,16,512]{4,3,2,1,0:T(8,128)(2,1)S(1)} %weigh.1), channel_id=1, replica_groups={{0,1,9,8,16,17,25,24},{2,3,11,10,18,19,27,26},{4,5,13,12,20,21,29,28},{..., dimensions={0} | all-to-all | bytes 3145728 | tf_op jit(solution)/shard_map/all_to_all | solution.py:194
  33.8 0.0 copy-start.5
  33.8 0.0 copy-done.1
  33.8 0.8 %contract.1 = (bf16[4,48,512]{2,1,0:T(8,128)(2,1)S(1)}, f32[4,48,512]{2,1,0:T(8,128)S(1)}) custom-call(bf16[8,4,3,16,512]{4,3,2,1,0:T(8,128)(2,1)S(1)} %all_to_all.21.rows_in, bf16[48,512]{1,0:T(8,128)(2,1)S(1)} %bitcast.17), custom_call_target="tpu_custom_call" | custom-call | tf_op jit(solution)/shard_map/contract/pallas_call | solution.py:197
  34.7 25.2 %all_to_all.22.parts = bf16[4,48,512]{2,1,0:T(8,128)(2,1)S(1)} all-to-all(bf16[4,48,512]{2,1,0:T(8,128)(2,1)S(1)} %get-tuple-element.9), channel_id=1, replica_groups={{0,2,4,6},{1,3,5,7},{8,10,12,14},{9,11,13,15},{16,18,20,22},{17,19,21,2..., dimensions={0} | all-to-all | bytes 393216 | tf_op jit(solution)/shard_map/all_to_all | solution.py:208
  59.8 0.0 copy-done.5
  59.8 1.9 %solve.1 = (f32[48,512]{1,0:T(8,128)S(1)}, f32[32,128]{1,0:T(8,128)S(1)}) custom-call(s32[32]{0:T(128)S(1)} %bitcast.23, s32[32]{0:T(128)S(1)} %bitcast.25, s32[32]{0:T(128)S(1)} %bitcast.26, bf16[4,48,512]{2,1,0:T(8,128)(2,1)S(1)} %all_to_all.22.parts, f32[4,48,512]{2,1,0:T(8,128)S(1)} %get-tuple-element.10.exact, bf16[48,512]{1,0:T(8,128)(2,1)S(1)} %bitcast.18), custom_call_target="tpu_custom_call" | custom-call | tf_op jit(solution)/shard_map/solve/pallas_call | solution.py:209
  61.8 18.6 %all_to_all.23 = f32[32,1,128]{2,1,0:T(1,128)S(1)} all-to-all(f32[32,1,128]{2,1,0:T(1,128)S(1)} %bitcast.20), channel_id=1, replica_groups=mesh['stretch'=16,'worker'=32] {'worker'}, dimensions={0} | all-to-all | bytes 32768 | tf_op jit(solution)/shard_map/all_to_all | solution.py:220
  80.4 0.7 finish.1
Async XLA Ops:
  0.0 5.3 %collective-permute-start = (f32[16,32]{1,0:T(8,128)}, f32[16,32]{1,0:T(8,128)S(1)}, u32[]{:S(2)}, u32[]{:S(2)}) collective-permute-start(f32[16,32]{1,0:T(8,128)} %bitcast.27), channel_id=1, source_target_pairs={{0,32},{32,64},{64,96},{96,128},{128,160},{160,192},{192,224},{224... | collective-permute-start | bytes 6152 | tf_op jit(solution)/shard_map/ppermute | solution.py:172
  1.9 1.4 %copy-start = (bf16[1,32,3,16,512]{4,3,2,1,0:T(8,128)(2,1)S(1)}, bf16[1,32,3,16,512]{4,3,2,1,0:T(8,128)(2,1)}, u32[]{:S(2)}) copy-start(bf16[1,32,3,16,512]{4,3,2,1,0:T(8,128)(2,1)} %param.7) | copy-start | bytes 4718596
  3.3 0.7 copy-start.2
  4.0 1.3 %copy-start.3 = (s32[1,32]{1,0:T(1,128)S(1)}, s32[1,32]{1,0:T(1,128)}, u32[]{:S(2)}) copy-start(s32[1,32]{1,0:T(1,128)} %param.12) | copy-start | bytes 388
  4.0 1.3 %copy-start.4 = (s32[1,32]{1,0:T(1,128)S(1)}, s32[1,32]{1,0:T(1,128)}, u32[]{:S(2)}) copy-start(s32[1,32]{1,0:T(1,128)} %param.10) | copy-start | bytes 388
  6.2 27.6 %copy-start.1 = (bf16[1,512,48]{1,2,0:T(8,128)(2,1)S(1)}, bf16[1,512,48]{1,2,0:T(8,128)(2,1)}, u32[]{:S(2)}) copy-start(bf16[1,512,48]{1,2,0:T(8,128)(2,1)} %param.13) | copy-start | bytes 147460
  33.8 26.0 %copy-start.5 = (s32[1,32]{1,0:T(1,128)S(1)}, s32[1,32]{1,0:T(1,128)}, u32[]{:S(2)}) copy-start(s32[1,32]{1,0:T(1,128)} %param.11) | copy-start | bytes 388
